TPU v7x, 512 devices: a whole 4x4x16 slice. The times are simulated.
512 devices in a mesh: grp: 64 (over x, z), dev: 8 (over y, core).
Axes of the slice: x: 4, y: 4, z: 16, core: 2. Of those that a mesh axis runs over, the one named last changes fastest.
Arguments:
- tokens: bfloat16 [32768, 768], P(('grp', 'dev')), may hold values from -6 to 6
- expert_ids: int32 [32768, 8], P(('grp', 'dev')), may hold values from 0 to 511, as said below
- gates: bfloat16 [32768, 8], P(('grp', 'dev')), may hold values from 0.099609375 to 0.5
- w_in: bfloat16 [512, 768, 1536], P(('grp', 'dev')), may hold values from -0.21875 to 0.21875
- w_out: bfloat16 [512, 1536, 768], P(('grp', 'dev')), may hold values from -0.15625 to 0.15625
Outputs:
- mixed: bfloat16 [32768, 768], P(('grp', 'dev'))
Inputs may be any that keep to these rules, and one draw needn't show every extreme that they name: `expert_ids`: row t lists 8 experts; columns 2 * k and 2 * k + 1 are two different experts of one group (experts g * 8 to g * 8 + 7 form group g), and the four groups of a row differ. The owner of token t is t // 64, and its dev index is the owner modulo 8. The tokens of one owner pick one group at most 12 times, and every owner reaches it for some group. The tokens whose owners share a dev index pick each group exactly 4 * 64 times in all and each expert at most 192 times; in every group one expert is picked 192 times by the tokens of every dev index.
All inputs are finite; a program needn't handle non-finite values.
Results may differ from a plain program's by a relative error of at most 0.0057.
Values may be sent and summed in bfloat16 or wider, within the bound.
A program may use at most 64 MiB of HBM per device.

v0:
```python
import jax
import jax.numpy as jnp
from jax import lax
from jax.sharding import PartitionSpec as P


def earlier_count(onehot):
    return jnp.cumsum(onehot, axis=0) - onehot


def contract_rows(left, right):
    return lax.dot_general(
        left,
        right,
        (((0,), (0,)), ((), ())),
        precision=lax.Precision.HIGHEST,
        preferred_element_type=jnp.float32,
    )


def expert_rows(slot_block, w_first, w_second):

    def one_block(rows_block):
        hidden = jnp.maximum(
            jnp.dot(rows_block, w_first, preferred_element_type=jnp.float32), 0.0
        ).astype(jnp.bfloat16)
        return jnp.dot(hidden, w_second, preferred_element_type=jnp.float32).astype(jnp.bfloat16)

    return lax.map(one_block, slot_block)


def seat_sources(seat_of, valid, seat_total):
    item_count = seat_of.shape[0]
    target_seat = jnp.where(valid, seat_of, seat_total)
    empty_seats = jnp.full((seat_total,), item_count, jnp.int32)
    return empty_seats.at[target_seat].set(jnp.arange(item_count, dtype=jnp.int32), mode="drop")


def per_device(tokens, expert_ids, gates, w_in, w_out):
    n_grp = lax.axis_size("grp")
    n_dev = lax.axis_size("dev")
    token_count, feature_width = tokens.shape
    cap_grp = min(token_count, 3 * ((4 * token_count + n_grp - 1) // n_grp))
    cap_exp = min(4 * token_count, 24 * token_count // n_dev)
    seat_total = n_dev * cap_exp
    zero_half = jnp.zeros((), jnp.bfloat16)
    w_first = w_in[0]
    w_second = w_out[0]
    pair_ids = expert_ids.reshape(token_count * 4, 2)
    pair_group = pair_ids[:, 0] // n_dev
    group_hot = (pair_group[:, None] == jnp.arange(n_grp)[None, :]).astype(jnp.int32)
    group_rank = jnp.sum(earlier_count(group_hot) * group_hot, axis=1)
    target = pair_group * cap_grp + group_rank
    slot_count = n_grp * cap_grp
    placed = (target[None, :] == jnp.arange(slot_count)[:, None]).astype(jnp.int32)
    token_hot = placed.reshape(slot_count, token_count, 4).sum(axis=2)
    rows_out = jnp.dot(
        token_hot.astype(jnp.bfloat16), tokens, preferred_element_type=jnp.float32
    ).astype(jnp.bfloat16)
    local_ids = pair_ids % n_dev
    picks_out = jnp.dot(placed, local_ids + 1) - 1
    gains_out = jnp.dot(
        placed.astype(jnp.bfloat16),
        gates.reshape(token_count * 4, 2),
        preferred_element_type=jnp.float32,
    ).astype(jnp.bfloat16)
    rows_in, picks_in, gains_in = (
        lax.all_to_all(
            rows_out.reshape(n_grp, cap_grp, feature_width),
            "grp",
            split_axis=0,
            concat_axis=0,
            tiled=True,
        ),
        lax.all_to_all(
            picks_out.reshape(n_grp, cap_grp, 2), "grp", split_axis=0, concat_axis=0, tiled=True
        ),
        lax.all_to_all(
            gains_out.reshape(n_grp, cap_grp, 2), "grp", split_axis=0, concat_axis=0, tiled=True
        ),
    )
    relay_rows = rows_in.reshape(slot_count, feature_width)
    relay_picks = picks_in.reshape(slot_count, 2)
    relay_gains = gains_in.reshape(slot_count, 2)
    live_count = 4 * token_count
    slot_live = (relay_picks[:, 0] >= 0).astype(jnp.int32)
    slot_order = jnp.cumsum(slot_live) - 1
    packed = (
        (slot_order[None, :] == jnp.arange(live_count)[:, None]) & (slot_live[None, :] > 0)
    ).astype(jnp.int32)
    packed_rows = jnp.dot(
        packed.astype(jnp.bfloat16), relay_rows, preferred_element_type=jnp.float32
    ).astype(jnp.bfloat16)
    packed_picks = jnp.dot(packed, relay_picks)
    packed_gains = jnp.dot(
        packed.astype(jnp.bfloat16), relay_gains, preferred_element_type=jnp.float32
    ).astype(jnp.bfloat16)
    group_rows, group_picks, group_gains = (
        lax.all_gather(packed_rows, "dev", axis=0, tiled=True),
        lax.all_gather(packed_picks, "dev", axis=0, tiled=True),
        lax.all_gather(packed_gains, "dev", axis=0, tiled=True),
    )
    gathered_count = group_rows.shape[0]
    chosen = jnp.sum((group_picks == lax.axis_index("dev")).astype(jnp.int32), axis=1)
    expert_seat = jnp.cumsum(chosen) - 1
    seat_source = seat_sources(expert_seat, chosen > 0, seat_total)
    seat_live = seat_source < gathered_count
    taken_rows = jnp.take(group_rows, jnp.minimum(seat_source, gathered_count - 1), axis=0)
    expert_in = jnp.where(seat_live[:, None], taken_rows, zero_half)
    expert_out = expert_rows(
        expert_in.reshape(n_dev, cap_exp, feature_width), w_first, w_second
    ).reshape(seat_total, feature_width)
    spread_rows = jnp.take(expert_out, jnp.clip(expert_seat, 0, seat_total - 1), axis=0)
    spread = jnp.where((chosen > 0)[:, None], spread_rows, zero_half)
    back = lax.all_to_all(
        spread.reshape(n_dev, live_count, feature_width),
        "dev",
        split_axis=0,
        concat_axis=0,
        tiled=True,
    )
    match = (packed_picks[None, :, :] == jnp.arange(n_dev)[:, None, None]).astype(jnp.float32)
    row_weights = jnp.sum(match * packed_gains.astype(jnp.float32)[None, :, :], axis=2)
    packed_sum = jnp.sum(row_weights[:, :, None] * back.astype(jnp.float32), axis=0)
    partial_value = contract_rows(packed.astype(jnp.float32), packed_sum)
    returned_sums = lax.all_to_all(
        partial_value.reshape(n_grp, cap_grp, feature_width),
        "grp",
        split_axis=0,
        concat_axis=0,
        tiled=True,
    )
    mixed = contract_rows(
        token_hot.astype(jnp.float32), returned_sums.reshape(slot_count, feature_width)
    )
    return mixed.astype(jnp.bfloat16)


def solution(mesh):
    return jax.shard_map(
        per_device,
        mesh=mesh,
        in_specs=(
            P(("grp", "dev"), None),
            P(("grp", "dev"), None),
            P(("grp", "dev"), None),
            P(("grp", "dev"), None, None),
            P(("grp", "dev"), None, None),
        ),
        out_specs=P(("grp", "dev"), None),
        check_vma=False,
    )
```

profile of v0, /device:TPU:6, one launch (start us, length us, event | category | flops | bytes accessed | tf_op | source)
XLA Modules:
  0.0 426.4 jit_solution(9296313556347692572)
XLA Ops:
  6.5 0.8 copy.40
  9.3 0.7 copy.43
  10.0 18.8 %all-to-all-start = ((s32[64,12,2]{1,2,0:T(2,128)}), s32[64,12,2]{1,2,0:T(2,128)S(1)}, u32[]{:S(2)}, u32[]{:S(2)}) async-start(s32[64,12,2]{1,2,0:T(2,128)} %copy.43), calls=%async_computation | async-start | bytes 131072 | tf_op jit(solution)/shard_map/all_to_all | solution.py:75
  29.8 1.3 reshape.303
  31.1 10.6 %all-to-all-done = s32[64,12,2]{1,2,0:T(2,128)S(1)} async-done(((s32[64,12,2]{1,2,0:T(2,128)}), s32[64,12,2]{1,2,0:T(2,128)S(1)}, u32[]{:S(2)}, u32[]{:S(2)}) %all-to-all-start) | async-done | bytes 6176 | tf_op jit(solution)/shard_map/all_to_all | solution.py:75
  41.7 6.4 %all-to-all-start.2 = ((bf16[64,12,768]{2,1,0:T(8,128)(2,1)}), bf16[64,12,768]{2,1,0:T(8,128)(2,1)S(1)}, u32[]{:S(2)}, u32[]{:S(2)}) async-start(bf16[64,12,768]{2,1,0:T(8,128)(2,1)} %reshape.303), calls=%async_computation.2 | async-start | bytes 3145728 | tf_op jit(solution)/shard_map/all_to_all | solution.py:68
  48.9 74.3 %all-to-all-done.2 = bf16[64,12,768]{2,1,0:T(8,128)(2,1)S(1)} async-done(((bf16[64,12,768]{2,1,0:T(8,128)(2,1)}), bf16[64,12,768]{2,1,0:T(8,128)(2,1)S(1)}, u32[]{:S(2)}, u32[]{:S(2)}) %all-to-all-start.2) | async-done | bytes 1179680 | tf_op jit(solution)/shard_map/all_to_all | solution.py:68
  123.5 1.3 convolution_convert_fusion.2
  125.4 0.6 copy.48
  126.0 6.9 %all-to-all-start.1 = ((bf16[64,12,2]{1,2,0:T(2,128)(2,1)}), bf16[64,12,2]{1,2,0:T(2,128)(2,1)S(1)}, u32[]{:S(2)}, u32[]{:S(2)}) async-start(bf16[64,12,2]{1,2,0:T(2,128)(2,1)} %copy.48), calls=%async_computation.1 | async-start | bytes 65536 | tf_op jit(solution)/shard_map/all_to_all | solution.py:78
  133.5 12.1 %all_gather.6 = s32[2048,2]{0,1:T(2,128)S(1)} all-gather(s32[256,2]{0,1:T(2,128)S(1)} %fusion.19), channel_id=1, replica_groups=mesh['grp'=64,'dev'=8] {'dev'}, dimensions={0}, use_global_device_ids=true | all-gather | bytes 18432 | tf_op jit(solution)/shard_map/all_gather | solution.py:100
  146.4 8.0 %scatter_custom_fusion = s32[1536]{0:T(1024)S(1)} fusion(s32[2048]{0:T(1024)S(1)} %bitcast.90, s32[2048]{0:T(1024)S(1)} %iota.29, s32[]{:T(128)} %constant.103.clone.1), kind=kCustom, calls=%fused_computation.109 | custom fusion | bytes 6148 | tf_op jit(solution)/shard_map/scatter | solution.py:36
  154.8 9.0 %gather_fusion = bf16[1536,768]{1,0:T(8,128)(2,1)} fusion(bf16[2048,768]{1,0:T(8,128)(2,1)} %all-gather.2.cloned.1.call-done, s32[2048]{0:T(1024)S(1)} %pad_clamp_fusion), kind=kCustom, calls=%fused_computation | custom fusion | bytes 4724736 | tf_op jit(solution)/shard_map/jit(_take)/gather | solution.py:108
  163.8 3.0 select_select_fusion.1
  166.8 29.7 %while.11 = (s32[]{:T(128)}, bf16[8,192,768]{2,1,0:T(8,128)(2,1)S(1)}, bf16[8,192,768]{2,1,0:T(8,128)(2,1)}, bf16[768,1536]{1,0:T(8,128)(2,1)}, bf16[1536,768]{1,0:T(8,128)(2,1)}) while((s32[]{:T(128)}, bf16[8,192,768]{2,1,0:T(8,128)(2,1)S(1)}, bf16[8,192,768]{2,1,0:T(8,128)(2,1)}, bf16[768,1536]{1,0:T(8,128)(2,1)}, ...), condition=%wide.region_12.13_spmd.clone, body=%wide.region_11.12_spmd.sunk.clone | while | flops 906706944 | bytes 5309509 | solution.py:29
  166.8 3.7 fusion.84
  170.5 3.7 fusion.84
  174.2 3.7 fusion.84
  177.9 3.7 fusion.84
  181.7 3.7 fusion.84
  185.4 3.7 fusion.84
  189.1 3.7 fusion.84
  192.8 3.7 fusion.84
  196.5 9.4 %gather_fusion.1 = bf16[2048,768]{1,0:T(8,128)(2,1)} fusion(bf16[1536,768]{1,0:T(8,128)(2,1)S(1)} %bitcast.82, s32[2048]{0:T(1024)S(1)} %broadcast_clamp_fusion), kind=kCustom, calls=%fused_computation.1 | custom fusion | bytes 6299648 | tf_op jit(solution)/shard_map/jit(_take)/gather | solution.py:113
  205.9 3.5 select_select_fusion
  209.3 3.8 all-to-all-start.3
  214.0 37.3 %all-to-all-done.3 = bf16[8,256,768]{2,1,0:T(8,128)(2,1)S(1)} async-done(((bf16[8,256,768]{2,1,0:T(8,128)(2,1)}), bf16[8,256,768]{2,1,0:T(8,128)(2,1)S(1)}, u32[]{:S(2)}, u32[]{:S(2)}) %all-to-all-start.3) | async-done | bytes 3145760 | tf_op jit(solution)/shard_map/all_to_all | solution.py:115
  252.0 2.2 fusion.12
  254.2 1.4 copy.51
  255.7 158.5 %all_to_all.25 = f32[64,12,768]{2,1,0:T(8,128)S(1)} all-to-all(f32[64,12,768]{2,1,0:T(8,128)S(1)} %copy.51), channel_id=1, replica_groups=mesh['grp'=64,'dev'=8] {'grp'}, dimensions={0} | all-to-all | bytes 4718592 | tf_op jit(solution)/shard_map/all_to_all | solution.py:126
  414.2 1.5 reshape.306
  415.7 3.9 convolution_convert_fusion.3
  (71 shorter events, 7.7 us)
Async XLA Ops:
  6.5 22.8 %copy-start = (bf16[64,768]{1,0:T(8,128)(2,1)S(1)}, bf16[64,768]{1,0:T(8,128)(2,1)}, u32[]{:S(2)}) copy-start(bf16[64,768]{1,0:T(8,128)(2,1)} %param.7) | copy-start | bytes 294916
  10.0 31.7 %all-to-all-start = ((s32[64,12,2]{1,2,0:T(2,128)}), s32[64,12,2]{1,2,0:T(2,128)S(1)}, u32[]{:S(2)}, u32[]{:S(2)}) async-start(s32[64,12,2]{1,2,0:T(2,128)} %copy.43), calls=%async_computation | async-start | bytes 131072 | tf_op jit(solution)/shard_map/all_to_all | solution.py:75
  41.7 81.5 %all-to-all-start.2 = ((bf16[64,12,768]{2,1,0:T(8,128)(2,1)}), bf16[64,12,768]{2,1,0:T(8,128)(2,1)S(1)}, u32[]{:S(2)}, u32[]{:S(2)}) async-start(bf16[64,12,768]{2,1,0:T(8,128)(2,1)} %reshape.303), calls=%async_computation.2 | async-start | bytes 3145728 | tf_op jit(solution)/shard_map/all_to_all | solution.py:68
  48.2 106.7 %all-gather.2.cloned.1.call-start = ((), (), s32[]{:S(2)}) async-start(), calls=%async_computation.5 | async-start | bytes 3538944 | tf_op jit(solution)/shard_map/all_gather | solution.py:99
  48.9 75.8 %copy-start.1 = (bf16[64,8]{0,1:T(8,128)(2,1)S(1)}, bf16[64,8]{0,1:T(8,128)(2,1)}, u32[]{:S(2)}) copy-start(bf16[64,8]{0,1:T(8,128)(2,1)} %param.9) | copy-start | bytes 3076
  126.0 83.3 %all-to-all-start.1 = ((bf16[64,12,2]{1,2,0:T(2,128)(2,1)}), bf16[64,12,2]{1,2,0:T(2,128)(2,1)S(1)}, u32[]{:S(2)}, u32[]{:S(2)}) async-start(bf16[64,12,2]{1,2,0:T(2,128)(2,1)} %copy.48), calls=%async_computation.1 | async-start | bytes 65536 | tf_op jit(solution)/shard_map/all_to_all | solution.py:78
  209.3 42.0 %all-to-all-start.3 = ((bf16[8,256,768]{2,1,0:T(8,128)(2,1)}), bf16[8,256,768]{2,1,0:T(8,128)(2,1)S(1)}, u32[]{:S(2)}, u32[]{:S(2)}) async-start(bf16[8,256,768]{2,1,0:T(8,128)(2,1)} %select_select_fusion), calls=%async_computation.3 | async-start | bytes 6291456 | tf_op jit(solution)/shard_map/all_to_all | solution.py:115
Sparse Core Ops, SparseCore 0:
  124.9 28.0 all-gather.1
where the time goes:
time: 427 us; the launch traced here: 426 us
  blocking collectives  171 us (40%)
  waiting for transfers between devices  122 us (29%)
  matrix products  38.9 us (9%)
  starting transfers between devices  36 us (8%)
  local copies, waits for them, and re-layouts  35.5 us (8%)
  between operations  13.7 us (3%)
  other arithmetic  9.29 us (2%)
    all_to_all x1, blocking collectives, per_device(): lax.all_to_all(partial_value.reshape(n_grp, cap_grp, feature_width), 'grp...  159 us
    all_to_all x1, waiting for transfers between devices, per_device(): lax.all_to_all(rows_out.reshape(n_grp, cap_grp, feature_width), 'grp', sp...  74.3 us
    all_to_all x1, waiting for transfers between devices, per_device(): lax.all_to_all(spread.reshape(n_dev, live_count, feature_width), 'dev', s...  37.3 us
    dot_general x8, matrix products, one_block(): jnp.dot(hidden, w_second, preferred_element_type=jnp.float32)  29.5 us
    all_to_all x1, starting transfers between devices, per_device(): lax.all_to_all(picks_out.reshape(n_grp, cap_grp, 2), 'grp', split_axis=0,...  18.8 us
    all_gather x1, blocking collectives, per_device(): lax.all_gather(packed_picks, 'dev', axis=0, tiled=True)  12.1 us
    all_to_all x1, waiting for transfers between devices, per_device(): lax.all_to_all(picks_out.reshape(n_grp, cap_grp, 2), 'grp', split_axis=0,...  10.6 us
    gather x1, local copies, waits for them, and re-layouts, per_device(): jnp.take(expert_out, jnp.clip(expert_seat, 0, seat_total - 1), axis=0)  9.38 us
  transfers between devices with their start and end apart: 5, of which 3 were waited for; matrix products, arithmetic and copies ran while one was open for 16% of the time, Pallas kernels for 0%

commit v1 on v0

v1 whole, which is shorter than its diff:
```python
import jax
import jax.numpy as jnp
from jax import lax
from jax.sharding import PartitionSpec as P

F32 = jnp.float32
BF16 = jnp.bfloat16
NX = 4
NZ = 16


def per_device(tokens, expert_ids, gates, w_in, w_out):
    n_dev = lax.axis_size("dev")
    count, width = tokens.shape
    cap = 4 * count
    z_sets = [[x * NZ + z for z in range(NZ)] for x in range(NX)]
    x_sets = [[x * NZ + z for x in range(NX)] for z in range(NZ)]
    me = lax.axis_index("grp")
    my_x, my_z = me // NZ, me % NZ
    mine = lax.axis_index("dev")

    pairs = expert_ids.reshape(count, 4, 2)
    gate_pairs = gates.reshape(count, 4, 2)
    meta = jnp.concatenate(
        [
            (pairs[:, :, 0] // n_dev).astype(BF16),
            (pairs[:, :, 0] % n_dev).astype(BF16),
            (pairs[:, :, 1] % n_dev).astype(BF16),
            gate_pairs[:, :, 0],
            gate_pairs[:, :, 1],
        ],
        axis=1,
    ).T
    column = lax.all_gather(tokens, "grp", axis_index_groups=z_sets, tiled=True)
    metas = lax.all_gather(meta, "grp")
    group = metas[:, 0:4, :].astype(jnp.int32)
    tri = (jnp.arange(count)[:, None] < jnp.arange(count)[None, :]).astype(BF16)
    owners = NX * NZ
    tri_o = (jnp.arange(owners)[:, None] < jnp.arange(owners)[None, :]).astype(F32)
    targets = jnp.arange(NX) * NZ + my_z
    match = (group[None] == targets[:, None, None, None]).astype(BF16)
    hit = jnp.sum(match, axis=2)
    within = jnp.dot(hit, tri, preferred_element_type=F32)
    totals = jnp.sum(hit.astype(F32), axis=2)
    base = jnp.dot(totals, tri_o, precision=lax.Precision.HIGHEST)
    place = jnp.where(hit > 0, within + base[:, :, None], -1.0).astype(jnp.int32)
    own = lax.dynamic_slice_in_dim(place, my_x * NZ, NZ, axis=1).reshape(NX, NZ * count)
    rows = jnp.arange(cap)
    select = (own[:, None, :] == rows[None, :, None]).astype(BF16).reshape(NX * cap, NZ * count)
    spread = jnp.dot(select, column, preferred_element_type=F32).astype(BF16)
    group_rows = lax.psum_scatter(
        spread, "grp", scatter_dimension=0, axis_index_groups=x_sets, tiled=True
    )
    all_rows = lax.all_gather(group_rows, "dev", tiled=True)

    place_me = lax.dynamic_index_in_dim(place, my_x, 0, keepdims=False).reshape(-1)
    match_me = lax.dynamic_index_in_dim(match, my_x, 0, keepdims=False)
    facts = jnp.stack(
        [jnp.sum(match_me * metas[:, 4 * i : 4 * i + 4, :], axis=1) for i in range(1, 5)], axis=-1
    ).reshape(owners * count, 4)
    seat = (place_me[None, :] == rows[:, None]).astype(BF16)
    row_facts = jnp.dot(seat, facts, preferred_element_type=F32).astype(BF16)
    all_facts = lax.all_gather(row_facts, "dev", tiled=True)
    who = mine.astype(BF16)
    weight = jnp.where(all_facts[:, 0] == who, all_facts[:, 2], 0).astype(F32) + jnp.where(
        all_facts[:, 1] == who, all_facts[:, 3], 0
    ).astype(F32)

    hidden = jnp.maximum(jnp.dot(all_rows, w_in[0], preferred_element_type=F32), 0.0).astype(BF16)
    out = jnp.dot(hidden, w_out[0], preferred_element_type=F32)
    out = (out * weight[:, None]).astype(BF16)
    group_sum = lax.psum_scatter(out, "dev", scatter_dimension=0, tiled=True)
    back = lax.all_gather(group_sum, "grp", axis_index_groups=x_sets, tiled=True)
    partial_sum = lax.dot_general(
        select, back, (((0,), (0,)), ((), ())), preferred_element_type=F32
    ).astype(BF16)
    return lax.psum_scatter(
        partial_sum, "grp", scatter_dimension=0, axis_index_groups=z_sets, tiled=True
    )


def solution(mesh):
    tok = P(("grp", "dev"), None)
    return jax.shard_map(
        per_device,
        mesh=mesh,
        in_specs=(tok, tok, tok, P(("grp", "dev"), None, None), P(("grp", "dev"), None, None)),
        out_specs=tok,
        check_vma=False,
    )
```

time: 427 us -> 360 us (0.84)
  waiting for transfers between devices: 122 us -> 206 us
  blocking collectives: 171 us -> 111 us
  starting transfers between devices: 36 us -> 0.2 us
  local copies, waits for them, and re-layouts: 35.5 us -> 2.17 us
  matrix products: 38.9 us -> 24.3 us
  other arithmetic: 9.29 us -> 2.88 us
    all_to_all x1 -> x0, blocking collectives: 159 us -> none  [per_device(): lax.all_to_all(partial_value.reshape(n_grp, cap_grp, feature_width), 'grp...]
    reduce_scatter x0 -> x3, waiting for transfers between devices: none -> 147 us  [the longest x1 73.1 us: per_device(): lax.psum_scatter(partial_sum, 'grp', scatter_dimension=0, axis_index_grou...]
    all_to_all x4 -> x0, waiting for transfers between devices: 122 us -> none  [the longest x1 74.3 us: per_device(): lax.all_to_all(rows_out.reshape(n_grp, cap_grp, feature_width), 'grp', sp...]
    all_gather x1 -> x2, blocking collectives: 12.1 us -> 111 us  [the longest x1 99.5 us: per_device(): metas = lax.all_gather(meta, 'grp')]
    all_gather x1 -> x3, waiting for transfers between devices: 0.02 us -> 58.8 us  [the longest x1 33.9 us: per_device(): lax.all_gather(group_sum, 'grp', axis_index_groups=x_sets, tiled=True)]
    all_to_all x4 -> x0, starting transfers between devices: 35.9 us -> none  [the longest x1 18.8 us: per_device(): lax.all_to_all(picks_out.reshape(n_grp, cap_grp, 2), 'grp', split_axis=0,...]
    gather x2 -> x0, local copies, waits for them, and re-layouts: 18.4 us -> none  [the longest x1 9.38 us: per_device(): jnp.take(expert_out, jnp.clip(expert_seat, 0, seat_total - 1), axis=0)]
    dot_general x16 -> x7, matrix products: 38.9 us -> 24.3 us  [the longest x1 7.32 us: per_device(): jnp.dot(all_rows, w_in[0], preferred_element_type=F32)]
  transfers between devices with their start and end apart: 5 -> 6, of which waited for: 3 -> 5; matrix products, arithmetic and copies ran while one was open for 16% -> 2% of each run, Pallas kernels for 0% -> 0%
where the time goes in v1:
time: 360 us
  waiting for transfers between devices  206 us (57%)
  blocking collectives  111 us (31%)
  matrix products  24.3 us (7%)
  between operations  13.6 us (4%)
    all_gather x1, blocking collectives, per_device(): metas = lax.all_gather(meta, 'grp')  99.5 us
    reduce_scatter x1, waiting for transfers between devices, per_device(): lax.psum_scatter(partial_sum, 'grp', scatter_dimension=0, axis_index_grou...  73.1 us
    reduce_scatter x1, waiting for transfers between devices, per_device(): group_sum = lax.psum_scatter(out, 'dev', scatter_dimension=0, tiled=True)  43.6 us
    all_gather x1, waiting for transfers between devices, per_device(): lax.all_gather(group_sum, 'grp', axis_index_groups=x_sets, tiled=True)  33.9 us
    reduce_scatter x1, waiting for transfers between devices, per_device(): lax.psum_scatter(spread, 'grp', scatter_dimension=0, axis_index_groups=x_...  29.8 us
    all_gather x1, waiting for transfers between devices, per_device(): all_rows = lax.all_gather(group_rows, 'dev', tiled=True)  24.9 us
    all_gather x1, blocking collectives, per_device(): all_facts = lax.all_gather(row_facts, 'dev', tiled=True)  11.5 us
    dot_general x1, matrix products, per_device(): jnp.dot(all_rows, w_in[0], preferred_element_type=F32)  7.32 us
  transfers between devices with their start and end apart: 6, of which 5 were waited for; matrix products, arithmetic and copies ran while one was open for 2% of the time, Pallas kernels for 0%

profile of v1, /device:TPU:6, one launch (start us, length us, event | category | flops | bytes accessed | tf_op | source)
XLA Modules:
  0.0 360.2 jit_solution(1277123264415232062)
XLA Ops:
  6.5 0.7 all-gather.6.cloned.1.call-update
  7.3 0.0 reduce-scatter.4.cloned.1.call-start
  7.4 0.8 fusion.32
  8.1 0.8 fusion.31
  8.9 0.1 concatenate.4
  9.0 99.5 %all-gather.1 = bf16[64,20,64]{2,1,0:T(8,128)(2,1)S(1)} all-gather(bf16[1,20,64]{2,1,0:T(8,128)(2,1)S(1)} %bitcast.41), channel_id=2, replica_groups=mesh['grp'=64,'dev'=8] {'grp'}, dimensions={0}, use_global_device_ids=true | all-gather | bytes 166400 | tf_op jit(solution)/shard_map/all_gather | solution.py:35
  108.5 0.5 fusion.30
  109.0 0.1 convert_reduce_fusion
  109.1 0.1 fusion.18
  109.2 0.2 fusion.5
  109.4 0.1 eq.70
  109.5 1.6 bitcast_compare_fusion
  111.1 4.7 %convolution_convert_fusion.1 = bf16[1024,768]{1,0:T(8,128)(2,1)} fusion(pred[1024,1024]{1,0:T(32,128)(4,1)} %bitcast_compare_fusion, bf16[1024,768]{1,0:T(8,128)(2,1)} %all-gather.6.cloned.1.call-done), kind=kOutput, calls=%fused_computation.9 | convolution fusion | flops 1611399168 | bytes 4194304 | tf_op jit(solution)/shard_map/dot_general | solution.py:50
  115.8 0.0 all-gather.8.cloned.1.call-start
  115.9 29.8 %reduce-scatter.4.cloned.1.call-done = bf16[256,768]{1,0:T(8,128)(2,1)} async-done(((bf16[1024,768]{1,0:T(8,128)(2,1)}), bf16[256,768]{1,0:T(8,128)(2,1)}) %reduce-scatter.4.cloned.1.call-update) | async-done | bytes 393232 | tf_op jit(solution)/shard_map/reduce_scatter | solution.py:51
  145.8 0.1 eq.77
  145.9 0.2 compare_convert_fusion
  146.1 0.4 fusion.10
  146.5 0.1 stack.15
  146.6 0.1 stack.17
  146.7 0.1 stack.16
  146.8 0.1 stack.18
  146.8 0.8 fusion.6
  147.7 11.5 %all_gather.22 = bf16[2048,4]{0,1:T(4,128)(2,1)S(1)} all-gather(bf16[256,4]{0,1:T(4,128)(2,1)S(1)} %fusion.6), channel_id=1, replica_groups=mesh['grp'=64,'dev'=8] {'dev'}, dimensions={0}, use_global_device_ids=true | all-gather | bytes 18432 | tf_op jit(solution)/shard_map/all_gather | solution.py:63
  159.2 24.9 %all-gather.8.cloned.1.call-done = bf16[2048,768]{1,0:T(8,128)(2,1)} async-done(((bf16[256,768]{1,0:T(8,128)(2,1)}), bf16[2048,768]{1,0:T(8,128)(2,1)}) %all-gather.8.cloned.1.call-update) | async-done | bytes 3145744 | tf_op jit(solution)/shard_map/all_gather | solution.py:54
  184.1 7.3 %maximum_convert_fusion = bf16[2048,1536]{1,0:T(8,128)(2,1)S(1)} fusion(bf16[2048,768]{1,0:T(8,128)(2,1)} %all-gather.8.cloned.1.call-done, bf16[1,768,1536]{2,1,0:T(8,128)(2,1)S(1)} %copy-done), kind=kOutput, calls=%fused_computation | convolution fusion | flops 4838129664 | bytes 11796480 | tf_op jit(solution)/shard_map/dot_general | solution.py:69
  191.4 6.4 %multiply_convert_fusion = bf16[2048,768]{1,0:T(8,128)(2,1)} fusion(bf16[2048,1536]{1,0:T(8,128)(2,1)S(1)} %maximum_convert_fusion, f32[2048]{0:T(1024)S(1)} %bitcast.46, bf16[1,1536,768]{2,1,0:T(8,128)(2,1)S(1)} %copy-done.2), kind=kOutput, calls=%fused_computation.1 | convolution fusion | flops 4834983936 | bytes 11804672 | tf_op jit(solution)/shard_map/dot_general | solution.py:70
  197.9 0.0 all-gather.10.cloned.1.call-start
  197.9 43.6 %reduce-scatter.6.cloned.1.call-done = bf16[256,768]{1,0:T(8,128)(2,1)} async-done(((bf16[2048,768]{1,0:T(8,128)(2,1)}), bf16[256,768]{1,0:T(8,128)(2,1)}) %reduce-scatter.6.cloned.1.call-update) | async-done | bytes 393232 | tf_op jit(solution)/shard_map/reduce_scatter | solution.py:72
  241.6 33.9 %all-gather.10.cloned.1.call-done = bf16[1024,768]{1,0:T(8,128)(2,1)} async-done(((bf16[256,768]{1,0:T(8,128)(2,1)}), bf16[1024,768]{1,0:T(8,128)(2,1)}) %all-gather.10.cloned.1.call-update) | async-done | bytes 1572880 | tf_op jit(solution)/shard_map/all_gather | solution.py:73
  275.4 4.8 %convolution_convert_fusion = bf16[1024,768]{1,0:T(8,128)(2,1)} fusion(pred[1024,1024]{1,0:T(32,128)(4,1)S(1)} %copy-done.1, bf16[1024,768]{1,0:T(8,128)(2,1)} %all-gather.10.cloned.1.call-done), kind=kOutput, calls=%fused_computation.8 | convolution fusion | flops 1611399168 | bytes 4194304 | tf_op jit(solution)/shard_map/dot_general | solution.py:74
  280.3 73.1 %reduce-scatter.8.cloned.1.call-done = bf16[64,768]{1,0:T(8,128)(2,1)} async-done(((bf16[1024,768]{1,0:T(8,128)(2,1)}), bf16[64,768]{1,0:T(8,128)(2,1)}) %reduce-scatter.8.cloned.1.call-update) | async-done | bytes 98320 | tf_op jit(solution)/shard_map/reduce_scatter | solution.py:77
  (24 shorter events, 0.3 us)
Async XLA Ops:
  6.5 177.6 %copy-start = (bf16[1,768,1536]{2,1,0:T(8,128)(2,1)S(1)}, bf16[1,768,1536]{2,1,0:T(8,128)(2,1)}, u32[]{:S(2)}) copy-start(bf16[1,768,1536]{2,1,0:T(8,128)(2,1)} %param.8) | copy-start | bytes 7077892
  6.5 104.6 %all-gather.6.cloned.1.call-start = ((), (), s32[]{:S(2)}) async-start(), calls=%async_computation.3 | async-start | bytes 1671168 | tf_op jit(solution)/shard_map/all_gather | solution.py:34
  7.3 138.5 %reduce-scatter.4.cloned.1.call-start = ((), (), s32[]{:S(2)}) async-start(), calls=%async_computation.4 | async-start | bytes 1966080 | tf_op jit(solution)/shard_map/reduce_scatter | solution.py:51
  115.8 68.3 %all-gather.8.cloned.1.call-start = ((), (), s32[]{:S(2)}) async-start(), calls=%async_computation.5 | async-start | bytes 3538944 | tf_op jit(solution)/shard_map/all_gather | solution.py:54
  145.7 95.8 %reduce-scatter.6.cloned.1.call-start = ((), (), s32[]{:S(2)}) async-start(), calls=%async_computation.6 | async-start | bytes 3538944 | tf_op jit(solution)/shard_map/reduce_scatter | solution.py:72
  184.1 7.3 %copy-start.2 = (bf16[1,1536,768]{2,1,0:T(8,128)(2,1)S(1)}, bf16[1,1536,768]{2,1,0:T(8,128)(2,1)}, u32[]{:S(2)}) copy-start(bf16[1,1536,768]{2,1,0:T(8,128)(2,1)} %param.9) | copy-start | bytes 7077892
  197.8 77.6 %copy-start.1 = (pred[1024,1024]{1,0:T(32,128)(4,1)S(1)}, pred[1024,1024]{1,0:T(32,128)(4,1)}, u32[]{:S(2)}) copy-start(pred[1024,1024]{1,0:T(32,128)(4,1)} %bitcast_compare_fusion) | copy-start | bytes 3145732
  197.9 77.6 %all-gather.10.cloned.1.call-start = ((), (), s32[]{:S(2)}) async-start(), calls=%async_computation.7 | async-start | bytes 1966080 | tf_op jit(solution)/shard_map/all_gather | solution.py:73
  241.5 111.8 %reduce-scatter.8.cloned.1.call-start = ((), (), s32[]{:S(2)}) async-start(), calls=%async_computation.8 | async-start | bytes 1671168 | tf_op jit(solution)/shard_map/reduce_scatter | solution.py:77
Sparse Core Ops, SparseCore 0:
  9.4 77.0 all-gather.5
  116.0 29.7 reduce-scatter.3
  147.8 36.2 all-gather.7
  198.0 43.4 reduce-scatter.5
  243.5 31.9 all-gather.9
  280.4 72.9 reduce-scatter.7

commit v2 on v1

v2 whole, which is shorter than its diff:
```python
import jax
import jax.numpy as jnp
from jax import lax
from jax.experimental import pallas as pl
from jax.experimental.pallas import tpu as pltpu
from jax.sharding import PartitionSpec as P

F32 = jnp.float32
BF16 = jnp.bfloat16
NX = 4
NY = 4
NZ = 16
TOK = 64
D = 768
FF = 1536
HALF = 384
CAP = 256
COPIES = 160
MESH = pl.DeviceIdType.MESH
NT = (((1,), (1,)), ((), ()))


def iota(shape, dim):
    return lax.broadcasted_iota(jnp.int32, shape, dim)


def ones_where(cond):
    return jnp.where(cond, 1.0, 0.0).astype(BF16)


def mm(a, b):
    return jnp.dot(a, b, preferred_element_type=F32)


def kernel(
    tok_ref,
    meta_ref,
    w1_hbm,
    w2_hbm,
    out_ref,
    w1,
    w2,
    column,
    metas,
    meta_x,
    places,
    facts_q,
    select,
    select_t,
    spread,
    mid,
    fin,
    rows,
    row_facts,
    outs,
    peer,
    back,
    partial_sum,
    ring_in,
    ring_out,
    load_sem,
    send_sem,
    recv_sem,
):
    grp, dev = lax.axis_index("grp"), lax.axis_index("dev")
    x, z = grp // NZ, lax.rem(grp, NZ)
    y, c = dev // 2, lax.rem(dev, 2)
    z_next = (x * NZ + lax.rem(z + 1, NZ), dev)
    z_prev = (x * NZ + lax.rem(z + NZ - 1, NZ), dev)
    x_next = (lax.rem(x + 1, NX) * NZ + z, dev)
    x_prev = (lax.rem(x + NX - 1, NX) * NZ + z, dev)
    y_next = (grp, lax.rem(y + 1, NY) * 2 + c)
    y_prev = (grp, lax.rem(y + NY - 1, NY) * 2 + c)
    twin = (grp, y * 2 + 1 - c)

    load1 = pltpu.make_async_copy(w1_hbm.at[0], w1, load_sem.at[0])
    load2 = pltpu.make_async_copy(w2_hbm.at[0], w2, load_sem.at[1])
    load1.start()
    load2.start()

    barrier = pltpu.get_barrier_semaphore()
    for neighbour in (z_next, z_prev, x_next, x_prev, y_next, y_prev, twin):
        pl.semaphore_signal(barrier, inc=1, device_id=neighbour, device_id_type=MESH)
    pl.semaphore_wait(barrier, 7)

    started = []

    def send(src, dst, to):
        k = len(started)
        copy = pltpu.make_async_remote_copy(
            src_ref=src,
            dst_ref=dst,
            send_sem=send_sem.at[k],
            recv_sem=recv_sem.at[k],
            device_id=to,
            device_id_type=MESH,
        )
        copy.start()
        started.append(copy)
        return copy

    def block(r, h):
        return column.at[pl.ds((r % NZ) * TOK + h * 32, 32)]

    def pass_on(step, before):
        made = {}
        for h in range(2):
            for way, to in ((1, z_next), (-1, z_prev)):
                if (h, way) in before:
                    before[h, way].wait_recv()
                if step == 8 and h != (way < 0):
                    continue
                held = -way * (step - 1)
                src = tok_ref.at[pl.ds(h * 32, 32)] if step == 1 else block(held, h)
                made[h, way] = send(src, block(held - way, h), to)
        return made

    tokens_in = pass_on(1, {})
    m_up = send(meta_ref, meta_x.at[0], x_next)
    m_down = send(meta_ref, meta_x.at[1], x_prev)
    column[0:TOK, :] = tok_ref[...]
    m_up.wait_recv()
    m_far = send(meta_x.at[0], meta_x.at[2], x_next)
    m_down.wait_recv()
    m_far.wait_recv()
    metas[0:16, :] = meta_ref[...] + meta_x[0] + meta_x[1] + meta_x[2]

    def bundle(r):
        return metas.at[pl.ds((r % NZ) * 16, 16)]

    def pass_meta(step):
        made = [send(bundle(-(step - 1)), bundle(-step), z_next)]
        if step < 8:
            made.append(send(bundle(step - 1), bundle(step), z_prev))
        return made

    metas_in = pass_meta(1)
    for step in range(2, 9):
        tokens_in = pass_on(step, tokens_in)
        for copy in metas_in:
            copy.wait_recv()
        metas_in = pass_meta(step)
    for copy in metas_in:
        copy.wait_recv()

    group_of = metas[:, 0:128].astype(F32)
    match = []
    for i in range(NX):
        target = lax.rem(x + i, NX) * NZ + z
        match.append(jnp.where(group_of == target.astype(F32), 1.0, 0.0))
    sum_k = ones_where(lax.shift_right_logical(iota((64, 256), 1), 2) == iota((64, 256), 0))
    hits = jnp.concatenate([mm(sum_k, m.astype(BF16)) for m in match], axis=0)
    hits_b = hits.astype(BF16)
    lane_r, lane_c = iota((128, 128), 0), iota((128, 128), 1)
    before = ones_where((lane_r < lane_c) & ((lane_r < 64) == (lane_c < 64)))
    counts = mm(hits_b, ones_where(lane_r < 64))
    own_r, own_c = iota((256, 256), 0), iota((256, 256), 1)
    earlier = ones_where(
        (own_c < own_r) & (lax.shift_right_logical(own_c, 6) == lax.shift_right_logical(own_r, 6))
    )
    place = jnp.where(hits > 0, mm(hits_b, before) + mm(earlier, counts.astype(BF16)), -1.0)
    place_b = place.astype(BF16)
    fold_r, fold_c = iota((32, 256), 0), iota((32, 256), 1)
    first = (
        lax.shift_right_logical(fold_r, 3) * 64 + jnp.bitwise_and(fold_r, 7) * 8 + x
    )
    low = iota((32, 128), 1) < 64
    own_places = jnp.where(
        low,
        mm(ones_where(fold_c == first), place_b),
        mm(ones_where(fold_c == first + 4), place_b),
    )
    places[0:32, :] = own_places

    row_id = iota((CAP, 128), 0).astype(F32)

    def build_select(i):
        for b in range(8):
            select[pl.ds(i * CAP, CAP), b * 128 : (b + 1) * 128] = ones_where(
                row_id == places[i * 8 + b : i * 8 + b + 1, :]
            )

    def spread_one(i):
        build_select(i)
        got = mm(select[pl.ds(i * CAP, CAP), :], column[...]).astype(BF16)
        spread[i, 0] = got[:, 0:HALF]
        spread[i, 1] = got[:, HALF:D]

    def top(r):
        return pl.ds(r * 128, 128)

    for i in (2,):
        build_select(i)
    for copy in tokens_in.values():
        copy.wait_recv()

    def reduce_first(buf, nxt, prv):
        return (
            [send(buf.at[2, 0, top(r)], mid.at[nxt[1], 0, top(r)], prv[0]) for r in range(2)],
            [send(buf.at[2, 1, top(r)], mid.at[nxt[1], 1, top(r)], nxt[0]) for r in range(2)],
        )

    def reduce_direct(buf, i, nxt, prv):
        if i == 3:
            return [send(buf.at[3, 1, top(r)], fin.at[nxt[1], 0, 1, top(r)], prv[0]) for r in range(2)]
        return [send(buf.at[1, 0, top(r)], fin.at[nxt[1], 1, 0, top(r)], nxt[0]) for r in range(2)]

    def reduce_merge(buf, firsts, nxt, prv):
        made = []
        for r in range(2):
            rr = slice(r * 128, (r + 1) * 128)
            firsts[0][r].wait_recv()
            buf[3, 0, rr, :] = (
                buf[3, 0, rr, :].astype(F32) + mid[nxt[1], 0, rr, :].astype(F32)
            ).astype(BF16)
            made.append(send(buf.at[3, 0, top(r)], fin.at[nxt[1], 0, 0, top(r)], prv[0]))
            firsts[1][r].wait_recv()
            buf[1, 1, rr, :] = (
                buf[1, 1, rr, :].astype(F32) + mid[nxt[1], 1, rr, :].astype(F32)
            ).astype(BF16)
            made.append(send(buf.at[1, 1, top(r)], fin.at[nxt[1], 1, 1, top(r)], nxt[0]))
        return made

    def reduce_sum(buf, which, h):
        return (
            buf[0, h].astype(F32) + fin[which, 0, h].astype(F32) + fin[which, 1, h].astype(F32)
        ).astype(BF16)

    xn, xp = (x_next, 0), (x_prev, 0)
    got = mm(select[pl.ds(2 * CAP, CAP), :], column[...]).astype(BF16)
    spread[2, 0] = got[:, 0:HALF]
    spread[2, 1] = got[:, HALF:D]
    firsts = reduce_first(spread, xn, xp)
    spread_one(3)
    finals = reduce_direct(spread, 3, xn, xp)
    spread_one(1)
    finals += reduce_direct(spread, 1, xn, xp)
    finals += reduce_merge(spread, firsts, xn, xp)
    spread_one(0)

    match_own = match[0].astype(BF16)
    fact_a = mm(sum_k, match_own * metas[:, 128:256]).astype(BF16)
    fact_b = mm(sum_k, match_own * metas[:, 256:384]).astype(BF16)
    swap = ones_where((lane_r + 64 == lane_c) | (lane_r == lane_c + 64))
    four = jnp.concatenate(
        [fact_a, mm(fact_a, swap).astype(BF16), fact_b, mm(fact_b, swap).astype(BF16)], axis=1
    )
    pick_r, pick_c = iota((32, 64), 0), iota((32, 64), 1)
    even, odd = ones_where(pick_c == 2 * pick_r), ones_where(pick_c == 2 * pick_r + 1)
    four_e, four_o = mm(even, four), mm(odd, four)
    place_own = place_b[0:64, :]
    places[32:64, :] = jnp.where(low, mm(even, place_own), mm(odd, place_own))
    stack = jnp.concatenate(
        [
            jnp.where(low, four_e[:, 0:128], four_o[:, 128:256]),
            jnp.where(low, four_e[:, 128:256], four_o[:, 0:128]),
            jnp.where(low, four_e[:, 256:384], four_o[:, 384:512]),
            jnp.where(low, four_e[:, 384:512], four_o[:, 256:384]),
        ],
        axis=0,
    ).astype(BF16)
    q_r, q_c = iota((256, 128), 0), iota((256, 128), 1)
    deal = ones_where(
        (jnp.bitwise_and(q_r, 7) == lax.shift_right_logical(q_c, 5))
        & (lax.shift_right_logical(q_r, 3) == jnp.bitwise_and(q_c, 31))
    )
    facts_q[...] = mm(deal, stack)

    def gather_facts(b, total):
        hot = ones_where(row_id == places[pl.ds(32 + b, 1), :])
        return total + lax.dot_general(
            facts_q[pl.ds(pl.multiple_of(b * 8, 8), 8), :].astype(BF16),
            hot,
            NT,
            preferred_element_type=F32,
        )

    row_facts[0, 0] = lax.fori_loop(0, 32, gather_facts, jnp.zeros((8, CAP), F32))

    eye = ones_where(lane_r == lane_c)
    places_t = lax.dot_general(eye, own_places.astype(BF16), NT, preferred_element_type=F32)
    lane_id = iota((128, CAP), 1).astype(F32)
    for i in range(NX):
        for b in range(8):
            k = i * 8 + b
            select_t[b * 128 : (b + 1) * 128, i * CAP : (i + 1) * CAP] = ones_where(
                lane_id == places_t[:, k : k + 1]
            )

    for copy in finals:
        copy.wait_recv()
    rows[0, 0, :, 0:HALF] = reduce_sum(spread, 0, 0)
    rows[0, 0, :, HALF:D] = reduce_sum(spread, 0, 1)

    up, down = [], []
    for r in range(2):
        up.append(send(rows.at[0, 0, top(r)], rows.at[3, 0, top(r)], y_next))
        down.append(send(rows.at[0, 0, top(1 - r)], rows.at[1, 0, top(1 - r)], y_prev))
    across = [send(rows.at[0, 0], rows.at[0, 1], twin), send(row_facts.at[0, 0], row_facts.at[0, 1], twin)]
    f_up = send(row_facts.at[0, 0], row_facts.at[3, 0], y_next)
    f_down = send(row_facts.at[0, 0], row_facts.at[1, 0], y_prev)

    eye_rows = ones_where(own_r == own_c)
    expert = dev.astype(F32)

    def feed_forward(i):
        block_in = rows[i].reshape(2 * CAP, D)

        def part(n, total):
            lo = pl.multiple_of(n * 512, 512)
            hidden = jnp.maximum(mm(block_in, w1[:, pl.ds(lo, 512)]), 0.0).astype(BF16)
            return total + mm(hidden, w2[pl.ds(lo, 512), :])

        total = lax.fori_loop(0, FF // 512, part, jnp.zeros((2 * CAP, D), F32))
        for core in range(2):
            f = row_facts[i, core]
            weight = jnp.where(f[0:1] == expert, f[2:3], 0.0) + jnp.where(f[1:2] == expert, f[3:4], 0.0)
            weight = jnp.broadcast_to(weight, (128, CAP)).astype(BF16)
            weight = lax.dot_general(eye_rows, weight, NT, preferred_element_type=F32)
            for n in range(6):
                outs[core, i, n // 3, :, (n % 3) * 128 : (n % 3 + 1) * 128] = (
                    total[core * CAP : (core + 1) * CAP, n * 128 : (n + 1) * 128] * weight
                ).astype(BF16)
        return send(outs.at[1, i], peer.at[i], twin)

    def join_cores(i, copy):
        copy.wait_recv()
        for h in range(2):
            outs[0, i, h] = (outs[0, i, h].astype(F32) + peer[i, h].astype(F32)).astype(BF16)

    load1.wait()
    load2.wait()
    for copy in across:
        copy.wait_recv()
    joins = {0: feed_forward(0)}
    far = []
    up[0].wait_recv()
    far.append(send(rows.at[3, 0, top(0)], rows.at[2, 0, top(0)], y_next))
    down[0].wait_recv()
    far.append(send(rows.at[1, 0, top(1)], rows.at[2, 0, top(1)], y_prev))
    f_up.wait_recv()
    far.append(send(row_facts.at[3, 0], row_facts.at[2, 0], y_next))
    up[1].wait_recv()
    across = {3: [send(rows.at[3, 0], rows.at[3, 1], twin), send(row_facts.at[3, 0], row_facts.at[3, 1], twin)]}
    down[1].wait_recv()
    f_down.wait_recv()
    across[1] = [send(rows.at[1, 0], rows.at[1, 1], twin), send(row_facts.at[1, 0], row_facts.at[1, 1], twin)]
    yn, yp = (y_next, 1), (y_prev, 1)
    out_own = outs.at[0]
    for copy in across[3]:
        copy.wait_recv()
    joins[3] = feed_forward(3)
    for copy in far:
        copy.wait_recv()
    across[2] = [send(rows.at[2, 0], rows.at[2, 1], twin), send(row_facts.at[2, 0], row_facts.at[2, 1], twin)]
    join_cores(3, joins[3])
    finals = reduce_direct(out_own, 3, yn, yp)
    for copy in across[1]:
        copy.wait_recv()
    joins[1] = feed_forward(1)
    for copy in across[2]:
        copy.wait_recv()
    join_cores(1, joins[1])
    finals += reduce_direct(out_own, 1, yn, yp)
    joins[2] = feed_forward(2)
    join_cores(2, joins[2])
    firsts = reduce_first(out_own, yn, yp)
    join_cores(0, joins[0])
    finals += reduce_merge(out_own, firsts, yn, yp)
    for copy in finals:
        copy.wait_recv()
    for h in range(2):
        back[0:CAP, h * HALF : (h + 1) * HALF] = reduce_sum(out_own, 1, h)

    def back_half(i, r):
        return back.at[pl.ds(i * CAP + r * 128, 128)]

    up, down, far = [], [], []
    for r in range(2):
        up.append(send(back_half(0, r), back_half(3, r), x_next))
        down.append(send(back_half(0, 1 - r), back_half(1, 1 - r), x_prev))
    up[0].wait_recv()
    far.append(send(back_half(3, 0), back_half(2, 0), x_next))
    down[0].wait_recv()
    far.append(send(back_half(1, 1), back_half(2, 1), x_prev))
    for copy in (up[1], down[1], *far):
        copy.wait_recv()

    def to_tokens(m, carry):
        at = pl.ds(pl.multiple_of(m * 256, 256), 256)
        partial_sum[at, :] = mm(select_t[at, :], back[...])
        return carry

    lax.fori_loop(0, 4, to_tokens, 0)

    arrived = {}
    for step in range(1, 9):
        current = {}
        for h in range(2):
            for w, way, to in ((0, -1, z_prev), (1, 1, z_next)):
                if step == 1 and h != w:
                    continue
                target = (way * (9 - step)) % NZ
                at = slice(target * TOK + h * 32, target * TOK + h * 32 + 32)
                value = partial_sum[at, :]
                if (w, h) in arrived:
                    arrived[w, h].wait_recv()
                    value = value + ring_in[w, step - 2, h * 32 : h * 32 + 32, :].astype(F32)
                ring_out[w, step - 1, h * 32 : h * 32 + 32, :] = value.astype(BF16)
                part = pl.ds(h * 32, 32)
                current[w, h] = send(ring_out.at[w, step - 1, part], ring_in.at[w, step - 1, part], to)
        arrived = current
    for copy in arrived.values():
        copy.wait_recv()
    out_ref[...] = (
        partial_sum[0:TOK, :] + ring_in[0, 7].astype(F32) + ring_in[1, 7].astype(F32)
    ).astype(BF16)

    for copy in started:
        copy.wait_send()


def per_device(tokens, expert_ids, gates, w_in, w_out):
    x = lax.axis_index("grp") // NZ
    pairs = expert_ids.reshape(TOK, 4, 2)
    gate_pairs = gates.reshape(TOK, 4, 2)
    group = (pairs[:, :, 0] // 8).astype(BF16)
    fields = jnp.stack(
        [
            group,
            group,
            (pairs[:, :, 0] % 8).astype(BF16),
            (pairs[:, :, 1] % 8).astype(BF16),
            gate_pairs[:, :, 0],
            gate_pairs[:, :, 1],
        ]
    )
    fields = fields.transpose(2, 0, 1).reshape(4, 6 * TOK)
    meta = jnp.where((jnp.arange(16) // 4 == x)[:, None], jnp.tile(fields, (4, 1)), 0)
    vmem = pl.BlockSpec(memory_space=pltpu.VMEM)
    hbm = pl.BlockSpec(memory_space=pl.ANY)
    return pl.pallas_call(
        kernel,
        out_shape=jax.ShapeDtypeStruct((TOK, D), BF16),
        in_specs=[vmem, vmem, hbm, hbm],
        out_specs=vmem,
        scratch_shapes=[
            pltpu.VMEM((D, FF), BF16),
            pltpu.VMEM((FF, D), BF16),
            pltpu.VMEM((NZ * TOK, D), BF16),
            pltpu.VMEM((NZ * 16, 384), BF16),
            pltpu.VMEM((3, 16, 384), BF16),
            pltpu.VMEM((64, 128), F32),
            pltpu.VMEM((256, 128), F32),
            pltpu.VMEM((NX * CAP, NZ * TOK), BF16),
            pltpu.VMEM((NZ * TOK, NX * CAP), BF16),
            pltpu.VMEM((4, 2, CAP, HALF), BF16),
            pltpu.VMEM((2, 2, CAP, HALF), BF16),
            pltpu.VMEM((2, 2, 2, CAP, HALF), BF16),
            pltpu.VMEM((4, 2, CAP, D), BF16),
            pltpu.VMEM((4, 2, 8, CAP), F32),
            pltpu.VMEM((2, 4, 2, CAP, HALF), BF16),
            pltpu.VMEM((4, 2, CAP, HALF), BF16),
            pltpu.VMEM((NX * CAP, D), BF16),
            pltpu.VMEM((NZ * TOK, D), F32),
            pltpu.VMEM((2, 8, TOK, D), BF16),
            pltpu.VMEM((2, 8, TOK, D), BF16),
            pltpu.SemaphoreType.DMA((2,)),
            pltpu.SemaphoreType.DMA((COPIES,)),
            pltpu.SemaphoreType.DMA((COPIES,)),
        ],
        compiler_params=pltpu.CompilerParams(
            collective_id=0, has_side_effects=True, vmem_limit_bytes=56 * 1024 * 1024
        ),
        cost_estimate=pl.CostEstimate(
            flops=15_000_000_000, bytes_accessed=5_000_000, transcendentals=0
        ),
    )(tokens, meta, w_in, w_out)


def solution(mesh):
    tok = P(("grp", "dev"), None)
    return jax.shard_map(
        per_device,
        mesh=mesh,
        in_specs=(tok, tok, tok, P(("grp", "dev"), None, None), P(("grp", "dev"), None, None)),
        out_specs=tok,
        check_vma=False,
    )
```

time: 360 us -> 150 us (0.42)
  waiting for transfers between devices: 206 us -> 0 us
  Pallas kernels: 0 us -> 145 us
  blocking collectives: 111 us -> 0 us
  matrix products: 24.3 us -> 0 us
  between operations: 13.6 us -> 0.03 us
    reduce_scatter x3 -> x0, waiting for transfers between devices: 147 us -> none  [the longest x1 73.1 us: per_device(): lax.psum_scatter(partial_sum, 'grp', scatter_dimension=0, axis_index_grou...]
    pallas_call x0 -> x1, Pallas kernels: none -> 145 us  [per_device(): pl.pallas_call(kernel, out_shape=jax.ShapeDtypeStruct((TOK, D), BF16), in...]
    all_gather x2 -> x0, blocking collectives: 111 us -> none  [the longest x1 99.5 us: per_device(): metas = lax.all_gather(meta, 'grp')]
    all_gather x3 -> x0, waiting for transfers between devices: 58.8 us -> none  [the longest x1 33.9 us: per_device(): lax.all_gather(group_sum, 'grp', axis_index_groups=x_sets, tiled=True)]
    dot_general x7 -> x0, matrix products: 24.3 us -> none  [the longest x1 7.32 us: per_device(): jnp.dot(all_rows, w_in[0], preferred_element_type=F32)]
  transfers between devices with their start and end apart: 6 -> 0, of which waited for: 5 -> 0; matrix products, arithmetic and copies ran while one was open for 2% -> 0% of each run, Pallas kernels for 0% -> 0%
where the time goes in v2:
time: 150 us; the launch traced here: 149 us
  Pallas kernels  145 us (97%)
  local copies, waits for them, and re-layouts  3.2 us (2%)
    pallas_call x1, Pallas kernels, per_device(): pl.pallas_call(kernel, out_shape=jax.ShapeDtypeStruct((TOK, D), BF16), in...  145 us

profile of v2, /device:TPU:6, one launch (start us, length us, event | category | flops | bytes accessed | tf_op | source)
XLA Modules:
  0.0 149.1 jit_solution(8688920054241081234)
XLA Ops:
  0.0 0.8 fusion.6
  0.8 0.8 fusion.7
  1.6 0.1 tile.10
  1.8 0.7 broadcast_select_fusion.meta_ref
  2.4 145.1 %shard_map.55 = bf16[64,768]{1,0:T(8,128)(2,1)} custom-call(bf16[64,768]{1,0:T(8,128)(2,1)} %tok_ref.1, bf16[16,384]{1,0:T(8,128)(2,1)} %broadcast_select_fusion.meta_ref, bf16[1,768,1536]{2,1,0:T(8,128)(2,1)} %w1_hbm.1, bf16[1,1536,768]{2,1,0:T(8,128)(2,1)} %w2_hbm.1), custom_call_target="tpu_custom_call" | custom-call | flops 15000000512 | bytes 5000000 | tf_op jit(solution)/shard_map/pallas_call | solution.py:442
  147.6 1.5 %copy.26 = bf16[64,768]{1,0:T(8,128)(2,1)} copy(bf16[64,768]{1,0:T(8,128)(2,1)} %shard_map.55) | data formatting | bytes 196608
  (10 shorter events, 0.1 us)

commit v3 on v2

v3 whole, which is shorter than its diff:
```python
import jax
import jax.numpy as jnp
from jax import lax
from jax.experimental import pallas as pl
from jax.experimental.pallas import tpu as pltpu
from jax.sharding import PartitionSpec as P

F32 = jnp.float32
BF16 = jnp.bfloat16
NX = 4
NY = 4
NZ = 16
TOK = 64
D = 768
FF = 1536
HALF = 384
CAP = 256
WIDE = 896
SLOT = 12
QUAD = 48
COPIES = 240
PIECES = 4
PIECE = 16
ORDER = (0, 1, -1, 2, -2, 3, -3, 4, -4, 5, -5, 6, -6, 7, -7, 8)
MESH = pl.DeviceIdType.MESH
NT = (((1,), (1,)), ((), ()))


def iota(shape, dim):
    return lax.broadcasted_iota(jnp.int32, shape, dim)


def ones_where(cond):
    return jnp.where(cond, 1.0, 0.0).astype(BF16)


def mm(a, b):
    return jnp.dot(a, b, preferred_element_type=F32)


def kernel(
    tok_ref,
    w1_hbm,
    w2_hbm,
    out_ref,
    w1,
    w2,
    column,
    slot_rows,
    select_t,
    stage,
    slots,
    earlier,
    unpack,
    mid,
    fin,
    rows,
    row_facts,
    outs,
    peer,
    sums,
    spread,
    back,
    partial_sum,
    ring_in,
    ring_out,
    load_sem,
    send_sem,
    recv_sem,
):
    grp, dev = lax.axis_index("grp"), lax.axis_index("dev")
    x, z = grp // NZ, lax.rem(grp, NZ)
    y, c = dev // 2, lax.rem(dev, 2)
    z_next = (x * NZ + lax.rem(z + 1, NZ), dev)
    z_prev = (x * NZ + lax.rem(z + NZ - 1, NZ), dev)
    x_next = (lax.rem(x + 1, NX) * NZ + z, dev)
    x_prev = (lax.rem(x + NX - 1, NX) * NZ + z, dev)
    y_next = (grp, lax.rem(y + 1, NY) * 2 + c)
    y_prev = (grp, lax.rem(y + NY - 1, NY) * 2 + c)
    twin = (grp, y * 2 + 1 - c)
    x_far = (lax.rem(x + 2, NX) * NZ + z, dev)

    load1 = pltpu.make_async_copy(w1_hbm.at[0], w1, load_sem.at[0])
    load2 = pltpu.make_async_copy(w2_hbm.at[0], w2, load_sem.at[1])
    load1.start()
    load2.start()

    barrier = pltpu.get_barrier_semaphore()
    for neighbour in (z_next, z_prev, x_next, x_prev, x_far, y_next, y_prev, twin):
        pl.semaphore_signal(barrier, inc=1, device_id=neighbour, device_id_type=MESH)
    pl.semaphore_wait(barrier, 8)

    started = []

    def send(src, dst, to):
        k = len(started)
        copy = pltpu.make_async_remote_copy(
            src_ref=src,
            dst_ref=dst,
            send_sem=send_sem.at[k],
            recv_sem=recv_sem.at[k],
            device_id=to,
            device_id_type=MESH,
        )
        copy.start()
        started.append(copy)
        return copy

    def block(r, h):
        at = ORDER.index(r if -7 <= r <= 8 else r % NZ)
        return column.at[pl.ds(at * TOK + h * PIECE, PIECE)]

    def pass_on(step, before):
        made = {}
        for h in range(PIECES):
            for way, to in ((1, z_next), (-1, z_prev)):
                if (h, way) in before:
                    before[h, way].wait_recv()
                if step > 8 or step == 8 and (h < PIECES // 2) == (way < 0):
                    continue
                held = -way * (step - 1)
                src = tok_ref.at[pl.ds(h * PIECE, PIECE)] if step == 1 else block(held, h)
                made[h, way] = send(src, block(held - way, h), to)
        return made

    tokens_in = pass_on(1, {})
    column[0:TOK, :] = tok_ref[...]

    lane_256 = iota((256, 256), 1)
    row_256 = iota((256, 256), 0)
    before_in_owner = ones_where(
        (row_256 < lane_256)
        & (lax.shift_right_logical(row_256, 6) == lax.shift_right_logical(lane_256, 6))
    )
    first_lanes = ones_where(iota((8, 128), 0) == iota((8, 128), 1))
    slot_base = (lax.shift_right_logical(iota((8, 256), 1), 6) * SLOT).astype(F32)
    slot_id = iota((QUAD, 256), 0).astype(F32)
    index_8 = iota((8, 256), 0)
    eye_rows = ones_where(row_256 == lane_256)
    x_ways = ((1, x_next, 3), (2, x_far, 2), (3, x_prev, 1))

    def quad(q, i):
        return pl.ds((q * NX + i) * QUAD, QUAD)

    def place_batch(q):
        at = slice(q * 256, q * 256 + 256)
        group_of = lax.dot_general(
            first_lanes, column[at, D:WIDE], NT, preferred_element_type=F32
        )
        hits = jnp.zeros((8, 256), F32)
        for i in range(NX):
            target = (lax.rem(x + i, NX) * NZ + z + 1).astype(F32)
            same = jnp.where(group_of == target, 1.0, 0.0)
            hit = same[0:1] + same[1:2] + same[2:3] + same[3:4]
            hits = jnp.where(index_8 == i, hit, hits)
        rank = mm(hits.astype(BF16), before_in_owner)
        slot = jnp.where(hits > 0, rank + slot_base, -1.0)
        slot_rows[q] = slot
        select = jnp.concatenate(
            [ones_where(slot_id == slot[i : i + 1]) for i in range(NX)], axis=0
        )
        got = mm(select, column[at, :]).astype(BF16)
        stage[q] = got
        slots[(q * NX) * QUAD : (q * NX) * QUAD + QUAD, :] = got[0:QUAD]
        return [
            send(stage.at[q, pl.ds(i * QUAD, QUAD)], slots.at[quad(q, there)], to)
            for i, to, there in (x_ways[1], x_ways[0], x_ways[2])
        ]

    def place_back(q):
        slot_t = lax.dot_general(
            eye_rows, slot_rows[q].astype(BF16), NT, preferred_element_type=F32
        )
        lane = iota((256, NX * QUAD), 1).astype(F32)
        hot = jnp.zeros((256, NX * QUAD), F32)
        for i in range(NX):
            col = slot_t[:, i : i + 1]
            hot = jnp.where((lane == col + float(i * QUAD)) & (col >= 0), 1.0, hot)
        select_t[q] = hot.astype(BF16)

    slots_in = []
    for step in range(2, 10):
        tokens_in = pass_on(step, tokens_in)
        if step == 2:
            for b in range(NX * NX * QUAD // 128):
                shape = (128, NX * NX * QUAD)
                earlier[b * 128 : (b + 1) * 128, :] = ones_where(
                    iota(shape, 1) < iota(shape, 0) + b * 128
                )
        if step in (3, 5, 7, 9):
            slots_in += place_batch(step // 2 - 1)
        if step in (4, 6, 8):
            place_back(step // 2 - 2)
    place_back(3)
    for copy in slots_in:
        copy.wait_recv()

    lane_r, lane_c = iota((128, 128), 0), iota((128, 128), 1)
    meta = slots[:, D:WIDE]
    lanes = iota((NX * NX * QUAD, 128), 1)
    match = ones_where((meta.astype(F32) == (grp + 1).astype(F32)) & (lanes < 4))
    repeat = ones_where((jnp.bitwise_and(lane_c, 3) == lane_r) & (lane_c < 20))
    live = mm(match, ones_where(lane_r < 4))
    chosen = (mm(match, repeat) * meta.astype(F32)).astype(BF16)
    facts = mm(
        chosen, ones_where((lax.shift_right_logical(lane_r, 2) == lane_c + 1) & (lane_r < 20))
    ).astype(BF16)
    place = jnp.where(live > 0, mm(earlier[...], live.astype(BF16)), -1.0)
    lane_f = lanes.astype(F32)
    unpack[:, 0:128] = ones_where(place == lane_f)
    unpack[:, 128:256] = ones_where(place == lane_f + 128.0)
    place_t = lax.dot_general(
        ones_where(iota((8, 128), 1) == 0), place.astype(BF16), NT, preferred_element_type=F32
    )
    pack = ones_where(iota((CAP, NX * NX * QUAD), 0).astype(F32) == place_t[0:1])
    rows[0, 0] = mm(pack, slots[:, 0:D]).astype(BF16)
    row_facts[0, 0] = lax.dot_general(
        first_lanes, mm(pack, facts).astype(BF16), NT, preferred_element_type=F32
    )

    def top(r):
        return pl.ds(r * 128, 128)

    def reduce_first(buf, nxt, prv):
        return (
            [send(buf.at[2, 0, top(r)], mid.at[0, top(r)], prv) for r in range(2)],
            [send(buf.at[2, 1, top(r)], mid.at[1, top(r)], nxt) for r in range(2)],
        )

    def reduce_direct(buf, i, nxt, prv):
        if i == 3:
            return [send(buf.at[3, 1, top(r)], fin.at[0, 1, top(r)], prv) for r in range(2)]
        return [send(buf.at[1, 0, top(r)], fin.at[1, 0, top(r)], nxt) for r in range(2)]

    def reduce_merge(buf, firsts, nxt, prv):
        made = []
        for r in range(2):
            rr = slice(r * 128, (r + 1) * 128)
            firsts[0][r].wait_recv()
            buf[3, 0, rr, :] = (
                buf[3, 0, rr, :].astype(F32) + mid[0, rr, :].astype(F32)
            ).astype(BF16)
            made.append(send(buf.at[3, 0, top(r)], fin.at[0, 0, top(r)], prv))
            firsts[1][r].wait_recv()
            buf[1, 1, rr, :] = (
                buf[1, 1, rr, :].astype(F32) + mid[1, rr, :].astype(F32)
            ).astype(BF16)
            made.append(send(buf.at[1, 1, top(r)], fin.at[1, 1, top(r)], nxt))
        return made

    def reduce_sum(buf, h):
        return (
            buf[0, h].astype(F32) + fin[0, h].astype(F32) + fin[1, h].astype(F32)
        ).astype(BF16)

    up, down = [], []
    for r in range(2):
        up.append(send(rows.at[0, 0, top(r)], rows.at[3, 0, top(r)], y_next))
        down.append(send(rows.at[0, 0, top(1 - r)], rows.at[1, 0, top(1 - r)], y_prev))
    across = [send(rows.at[0, 0], rows.at[0, 1], twin), send(row_facts.at[0, 0], row_facts.at[0, 1], twin)]
    f_up = send(row_facts.at[0, 0], row_facts.at[3, 0], y_next)
    f_down = send(row_facts.at[0, 0], row_facts.at[1, 0], y_prev)

    expert = dev.astype(F32)

    def feed_forward(i):
        block_in = rows[i].reshape(2 * CAP, D)

        def part(n, total):
            lo = pl.multiple_of(n * 512, 512)
            hidden = jnp.maximum(mm(block_in, w1[:, pl.ds(lo, 512)]), 0.0).astype(BF16)
            return total + mm(hidden, w2[pl.ds(lo, 512), :])

        total = lax.fori_loop(0, FF // 512, part, jnp.zeros((2 * CAP, D), F32))
        for core in range(2):
            f = row_facts[i, core]
            weight = jnp.where(f[0:1] == expert, f[2:3], 0.0) + jnp.where(f[1:2] == expert, f[3:4], 0.0)
            weight = jnp.broadcast_to(weight, (128, CAP)).astype(BF16)
            weight = lax.dot_general(eye_rows, weight, NT, preferred_element_type=F32)
            for n in range(6):
                outs[core, i, n // 3, :, (n % 3) * 128 : (n % 3 + 1) * 128] = (
                    total[core * CAP : (core + 1) * CAP, n * 128 : (n + 1) * 128] * weight
                ).astype(BF16)
        return send(outs.at[1, i], peer.at[i], twin)

    def join_cores(i, copy):
        copy.wait_recv()
        for h in range(2):
            outs[0, i, h] = (outs[0, i, h].astype(F32) + peer[i, h].astype(F32)).astype(BF16)

    load1.wait()
    load2.wait()
    for copy in across:
        copy.wait_recv()
    joins = {0: feed_forward(0)}
    far = []
    up[0].wait_recv()
    far.append(send(rows.at[3, 0, top(0)], rows.at[2, 0, top(0)], y_next))
    down[0].wait_recv()
    far.append(send(rows.at[1, 0, top(1)], rows.at[2, 0, top(1)], y_prev))
    f_up.wait_recv()
    far.append(send(row_facts.at[3, 0], row_facts.at[2, 0], y_next))
    up[1].wait_recv()
    across = {3: [send(rows.at[3, 0], rows.at[3, 1], twin), send(row_facts.at[3, 0], row_facts.at[3, 1], twin)]}
    down[1].wait_recv()
    f_down.wait_recv()
    across[1] = [send(rows.at[1, 0], rows.at[1, 1], twin), send(row_facts.at[1, 0], row_facts.at[1, 1], twin)]
    yn, yp = y_next, y_prev
    out_own = outs.at[0]
    for copy in across[3]:
        copy.wait_recv()
    joins[3] = feed_forward(3)
    for copy in far:
        copy.wait_recv()
    across[2] = [send(rows.at[2, 0], rows.at[2, 1], twin), send(row_facts.at[2, 0], row_facts.at[2, 1], twin)]
    join_cores(3, joins[3])
    finals = reduce_direct(out_own, 3, yn, yp)
    for copy in across[1]:
        copy.wait_recv()
    joins[1] = feed_forward(1)
    for copy in across[2]:
        copy.wait_recv()
    join_cores(1, joins[1])
    finals += reduce_direct(out_own, 1, yn, yp)
    joins[2] = feed_forward(2)
    join_cores(2, joins[2])
    firsts = reduce_first(out_own, yn, yp)
    join_cores(0, joins[0])
    finals += reduce_merge(out_own, firsts, yn, yp)
    for copy in finals:
        copy.wait_recv()
    for h in range(2):
        sums[:, h * HALF : (h + 1) * HALF] = reduce_sum(out_own, h)

    back_in = {}
    for q in range(NX - 1, -1, -1):
        at = slice(q * NX * QUAD, (q + 1) * NX * QUAD)
        got = mm(unpack[at, :], sums[...]).astype(BF16)
        spread[q] = got
        back[q, 0:QUAD, :] = got[0:QUAD]
        back_in[q] = [
            send(spread.at[q, pl.ds(i * QUAD, QUAD)], back.at[q, pl.ds(there * QUAD, QUAD)], to)
            for i, to, there in (x_ways[1], x_ways[0], x_ways[2])
        ]

    ready = set()

    def own_part(r, h):
        at = ORDER.index(r)
        q = at // 4
        if q not in ready:
            ready.add(q)
            for copy in back_in[q]:
                copy.wait_recv()
            partial_sum[q * 256 : (q + 1) * 256, :] = mm(select_t[q], back[q])
        return partial_sum[at * TOK + h * PIECE : at * TOK + (h + 1) * PIECE, :]

    arrived = {}
    for step in range(1, 9):
        current = {}
        for h in range(PIECES):
            part = pl.ds(h * PIECE, PIECE)
            for w, way, to in ((0, -1, z_prev), (1, 1, z_next)):
                if step == 1 and (h < PIECES // 2) != (w == 0):
                    continue
                value = own_part(8 if step == 1 else way * (9 - step), h)
                if (w, h) in arrived:
                    arrived[w, h].wait_recv()
                    value = value + ring_in[w, step - 2, h * PIECE : (h + 1) * PIECE, :].astype(F32)
                ring_out[w, step - 1, h * PIECE : (h + 1) * PIECE, :] = value.astype(BF16)
                current[w, h] = send(ring_out.at[w, step - 1, part], ring_in.at[w, step - 1, part], to)
        arrived = current
    for copy in arrived.values():
        copy.wait_recv()
    out_ref[...] = (
        partial_sum[0:TOK, :] + ring_in[0, 7].astype(F32) + ring_in[1, 7].astype(F32)
    ).astype(BF16)

    for copy in started:
        copy.wait_send()


def per_device(tokens, expert_ids, gates, w_in, w_out):
    pairs = expert_ids.reshape(TOK, 4, 2)
    gate_pairs = gates.reshape(TOK, 4, 2)
    tokens = jnp.concatenate(
        [
            tokens,
            (pairs[:, :, 0] // 8 + 1).astype(BF16),
            (pairs[:, :, 0] % 8).astype(BF16),
            (pairs[:, :, 1] % 8).astype(BF16),
            gate_pairs[:, :, 0],
            gate_pairs[:, :, 1],
            jnp.zeros((TOK, 108), BF16),
        ],
        axis=1,
    )
    vmem = pl.BlockSpec(memory_space=pltpu.VMEM)
    hbm = pl.BlockSpec(memory_space=pl.ANY)
    return pl.pallas_call(
        kernel,
        out_shape=jax.ShapeDtypeStruct((TOK, D), BF16),
        in_specs=[vmem, hbm, hbm],
        out_specs=vmem,
        scratch_shapes=[
            pltpu.VMEM((D, FF), BF16),
            pltpu.VMEM((FF, D), BF16),
            pltpu.VMEM((NZ * TOK, WIDE), BF16),
            pltpu.VMEM((NX, 8, 256), F32),
            pltpu.VMEM((NX, 256, NX * QUAD), BF16),
            pltpu.VMEM((NX, NX * QUAD, WIDE), BF16),
            pltpu.VMEM((NX * NX * QUAD, WIDE), BF16),
            pltpu.VMEM((NX * NX * QUAD, NX * NX * QUAD), BF16),
            pltpu.VMEM((NX * NX * QUAD, CAP), BF16),
            pltpu.VMEM((2, CAP, HALF), BF16),
            pltpu.VMEM((2, 2, CAP, HALF), BF16),
            pltpu.VMEM((4, 2, CAP, D), BF16),
            pltpu.VMEM((4, 2, 8, CAP), F32),
            pltpu.VMEM((2, 4, 2, CAP, HALF), BF16),
            pltpu.VMEM((4, 2, CAP, HALF), BF16),
            pltpu.VMEM((CAP, D), BF16),
            pltpu.VMEM((NX, NX * QUAD, D), BF16),
            pltpu.VMEM((NX, NX * QUAD, D), BF16),
            pltpu.VMEM((NZ * TOK, D), F32),
            pltpu.VMEM((2, 8, TOK, D), BF16),
            pltpu.VMEM((2, 8, TOK, D), BF16),
            pltpu.SemaphoreType.DMA((2,)),
            pltpu.SemaphoreType.DMA((COPIES,)),
            pltpu.SemaphoreType.DMA((COPIES,)),
        ],
        compiler_params=pltpu.CompilerParams(
            collective_id=0, has_side_effects=True, vmem_limit_bytes=56 * 1024 * 1024
        ),
        cost_estimate=pl.CostEstimate(
            flops=15_000_000_000, bytes_accessed=5_000_000, transcendentals=0
        ),
    )(tokens, w_in, w_out)


def solution(mesh):
    tok = P(("grp", "dev"), None)
    return jax.shard_map(
        per_device,
        mesh=mesh,
        in_specs=(tok, tok, tok, P(("grp", "dev"), None, None), P(("grp", "dev"), None, None)),
        out_specs=tok,
        check_vma=False,
    )
```

time: 150 us -> 133 us (0.89)
  Pallas kernels: 145 us -> 126 us
  local copies, waits for them, and re-layouts: 3.2 us -> 5.12 us
    pallas_call x1, Pallas kernels: 145 us -> 126 us  [per_device(): pl.pallas_call(kernel, out_shape=jax.ShapeDtypeStruct((TOK, D), BF16), in...]
    concatenate x0 -> x1, local copies, waits for them, and re-layouts: none -> 1.63 us  [per_device(): jnp.concatenate([tokens, (pairs[:, :, 0] // 8 + 1).astype(BF16), (pairs[:...]
where the time goes in v3:
time: 133 us; the launch traced here: 132 us
  Pallas kernels  126 us (95%)
  local copies, waits for them, and re-layouts  5.12 us (4%)
    pallas_call x1, Pallas kernels, per_device(): pl.pallas_call(kernel, out_shape=jax.ShapeDtypeStruct((TOK, D), BF16), in...  126 us

profile of v3, /device:TPU:6, one launch (start us, length us, event | category | flops | bytes accessed | tf_op | source)
XLA Modules:
  0.0 131.7 jit_solution(11554939790170178476)
XLA Ops:
  0.0 0.8 fusion.8
  0.8 0.8 fusion.9
  1.5 0.1 copy.13
  1.6 0.1 copy.12
  1.8 0.1 copy.11
  1.9 0.1 copy.10
  1.9 0.1 fusion.2
  2.0 1.6 %concatenate.3.tok_ref = bf16[64,896]{1,0:T(8,128)(2,1)} concatenate(bf16[64,768]{1,0:T(8,128)(2,1)} %param.5, bf16[64,4]{1,0:T(8,128)(2,1)S(1)} %get-tuple-element.6, bf16[64,4]{1,0:T(8,128)(2,1)S(1)} %get-tuple-element.5, bf16[64,4]{1,0:T(8,128)(2,1)S(1)} %get-tuple-element.11, bf16[64,4]{1,0:T(8,128)(2,1)S(1)} %bitcast.35, bf16[64,4]{1,0:T(8,128)(2,1)S(1)} %bitcast.34, ...), dimensions={1} | concatenate | bytes 229376 | tf_op jit(solution)/shard_map/concatenate | solution.py:386
  3.6 126.5 %shard_map.55 = bf16[64,768]{1,0:T(8,128)(2,1)} custom-call(bf16[64,896]{1,0:T(8,128)(2,1)} %concatenate.3.tok_ref, bf16[1,768,1536]{2,1,0:T(8,128)(2,1)} %w1_hbm.1, bf16[1,1536,768]{2,1,0:T(8,128)(2,1)} %w2_hbm.1), custom_call_target="tpu_custom_call" | custom-call | flops 15000000512 | bytes 5000000 | tf_op jit(solution)/shard_map/pallas_call | solution.py:400
  130.1 1.5 %copy.15 = bf16[64,768]{1,0:T(8,128)(2,1)} copy(bf16[64,768]{1,0:T(8,128)(2,1)} %shard_map.55) | data formatting | bytes 196608
  (1 shorter events, 0.0 us)

commit v4 on v3

v4 whole, which is shorter than its diff:
```python
import jax
import jax.numpy as jnp
from jax import lax
from jax.experimental import pallas as pl
from jax.experimental.pallas import tpu as pltpu
from jax.sharding import PartitionSpec as P

F32 = jnp.float32
BF16 = jnp.bfloat16
NX = 4
NY = 4
NZ = 16
TOK = 64
D = 768
FF = 1536
HIDE = 512
CAP = 256
WIDE = 896
SLOT = 12
QUAD = 48
COPIES = 240
PIECES = 4
PIECE = 16
BATCHES = ((0, 4, 48), (4, 4, 48), (8, 4, 48), (12, 3, 48), (15, 1, 16))
BULK = 768
SLOTS = 832
ORDER = (0, 1, -1, 2, -2, 3, -3, 4, -4, 5, -5, 6, -6, 7, -7, 8)
MESH = pl.DeviceIdType.MESH
NT = (((1,), (1,)), ((), ()))


def iota(shape, dim):
    return lax.broadcasted_iota(jnp.int32, shape, dim)


def ones_where(cond):
    return jnp.where(cond, 1.0, 0.0).astype(BF16)


def mm(a, b):
    return jnp.dot(a, b, preferred_element_type=F32)


def kernel(
    tok_ref,
    ids_ref,
    gates_ref,
    w1_hbm,
    w2_hbm,
    out_ref,
    w1,
    w2,
    column,
    slot_rows,
    select_t,
    stage,
    slots,
    earlier,
    unpack,
    fin,
    lhs,
    hid,
    gain,
    rows,
    row_facts,
    outs,
    peer,
    sums,
    spread,
    back,
    partial_sum,
    ring_in,
    ring_out,
    load_sem,
    send_sem,
    recv_sem,
):
    grp, dev = lax.axis_index("grp"), lax.axis_index("dev")
    x, z = grp // NZ, lax.rem(grp, NZ)
    y, c = dev // 2, lax.rem(dev, 2)
    z_next = (x * NZ + lax.rem(z + 1, NZ), dev)
    z_prev = (x * NZ + lax.rem(z + NZ - 1, NZ), dev)
    x_next = (lax.rem(x + 1, NX) * NZ + z, dev)
    x_prev = (lax.rem(x + NX - 1, NX) * NZ + z, dev)
    y_next = (grp, lax.rem(y + 1, NY) * 2 + c)
    y_prev = (grp, lax.rem(y + NY - 1, NY) * 2 + c)
    twin = (grp, y * 2 + 1 - c)
    y_far = (grp, lax.rem(y + 2, NY) * 2 + c)
    x_far = (lax.rem(x + 2, NX) * NZ + z, dev)

    load1 = pltpu.make_async_copy(w1_hbm.at[0], w1, load_sem.at[0])
    load2 = pltpu.make_async_copy(w2_hbm.at[0], w2, load_sem.at[1])
    load1.start()
    load2.start()

    barrier = pltpu.get_barrier_semaphore()
    for neighbour in (z_next, z_prev, x_next, x_prev, x_far, y_next, y_prev, y_far, twin):
        pl.semaphore_signal(barrier, inc=1, device_id=neighbour, device_id_type=MESH)

    ids = ids_ref[...]
    to_r, to_c = iota((8, 128), 0), iota((8, 128), 1)
    column[0:TOK, 0:D] = tok_ref[...]
    column[0:TOK, D:WIDE] = (
        mm(
            (lax.shift_right_logical(ids, 3) + 1).astype(F32).astype(BF16),
            ones_where((to_r == 2 * to_c) & (to_c < 4)),
        )
        + mm(
            jnp.bitwise_and(ids, 7).astype(F32).astype(BF16),
            ones_where(
                ((to_r == 2 * (to_c - 4)) & (to_c < 8)) | ((to_r == 2 * (to_c - 8) + 1) & (to_c < 12))
            ),
        )
        + mm(
            gates_ref[...],
            ones_where(
                ((to_r == 2 * (to_c - 12)) & (to_c < 16)) | ((to_r == 2 * (to_c - 16) + 1) & (to_c < 20))
            ),
        )
    ).astype(BF16)
    pl.semaphore_wait(barrier, 9)

    started = []

    def send(src, dst, to):
        k = len(started)
        copy = pltpu.make_async_remote_copy(
            src_ref=src,
            dst_ref=dst,
            send_sem=send_sem.at[k],
            recv_sem=recv_sem.at[k],
            device_id=to,
            device_id_type=MESH,
        )
        copy.start()
        started.append(copy)
        return copy

    def block(r, h):
        at = ORDER.index(r if -7 <= r <= 8 else r % NZ)
        return column.at[pl.ds(at * TOK + h * PIECE, PIECE)]

    def pass_on(step, before):
        made = {}
        for h in range(PIECES):
            for way, to in ((1, z_next), (-1, z_prev)):
                if (h, way) in before:
                    before[h, way].wait_recv()
                if step > 8 or step == 8 and (h < PIECES // 2) == (way < 0):
                    continue
                held = -way * (step - 1)
                made[h, way] = send(block(held, h), block(held - way, h), to)
        return made

    tokens_in = pass_on(1, {})
    first_lanes = ones_where(iota((8, 128), 0) == iota((8, 128), 1))
    x_ways = ((2, x_far, 2), (1, x_next, 3), (3, x_prev, 1))

    def eye(n):
        return ones_where(iota((n, n), 0) == iota((n, n), 1))

    def place_batch(q):
        at, owners, part = BATCHES[q]
        n = owners * TOK
        tokens = slice(at * TOK, at * TOK + n)
        group_of = lax.dot_general(
            first_lanes, column[tokens, D:WIDE], NT, preferred_element_type=F32
        )
        hits = jnp.zeros((8, n), F32)
        for i in range(NX):
            target = (lax.rem(x + i, NX) * NZ + z + 1).astype(F32)
            same = jnp.where(group_of == target, 1.0, 0.0)
            hit = same[0:1] + same[1:2] + same[2:3] + same[3:4]
            hits = jnp.where(iota((8, n), 0) == i, hit, hits)
        r, l = iota((n, n), 0), iota((n, n), 1)
        before = ones_where(
            (r < l) & (lax.shift_right_logical(r, 6) == lax.shift_right_logical(l, 6))
        )
        base = (lax.shift_right_logical(iota((8, n), 1), 6) * SLOT).astype(F32)
        slot = jnp.where(hits > 0, mm(hits.astype(BF16), before) + base, -1.0)
        slot_rows[q, :, 0:n] = slot
        slot_id = iota((part, n), 0).astype(F32)
        select = jnp.concatenate(
            [ones_where(slot_id == slot[i : i + 1]) for i in range(NX)], axis=0
        )
        got = mm(select, column[tokens, :]).astype(BF16)
        stage[q, 0 : NX * part, :] = got
        lo = q * NX * QUAD
        slots[lo : lo + part, :] = got[0:part]
        return [
            send(
                stage.at[q, pl.ds(i * part, part)], slots.at[pl.ds(lo + there * part, part)], to
            )
            for i, to, there in x_ways
        ]

    def place_back(q):
        owners, part = BATCHES[q][1:]
        n = owners * TOK
        slot_t = lax.dot_general(
            eye(n), slot_rows[q, :, 0:n].astype(BF16), NT, preferred_element_type=F32
        )
        lane = iota((n, NX * part), 1).astype(F32)
        hot = jnp.zeros((n, NX * part), F32)
        for i in range(NX):
            col = slot_t[:, i : i + 1]
            hot = jnp.where((lane == col + float(i * part)) & (col >= 0), 1.0, hot)
        select_t[q, 0:n, 0 : NX * part] = hot.astype(BF16)

    slots_in = {}
    for step in range(2, 10):
        tokens_in = pass_on(step, tokens_in)
        if step == 2:
            for b in range(BULK // 128):
                shape = (128, BULK)
                earlier[b * 128 : (b + 1) * 128, :] = ones_where(
                    iota(shape, 1) < iota(shape, 0) + b * 128
                )
        if step in (3, 5, 7, 8, 9):
            q = (3, 5, 7, 8, 9).index(step)
            slots_in[q] = place_batch(q)
        if step in (4, 6):
            place_back(step // 2 - 2)
    place_back(2)
    for q in range(4):
        for copy in slots_in[q]:
            copy.wait_recv()

    lane_r, lane_c = iota((128, 128), 0), iota((128, 128), 1)
    repeat = ones_where((jnp.bitwise_and(lane_c, 3) == lane_r) & (lane_c < 20))
    first_four = ones_where(lane_r < 4)
    to_facts = ones_where((lax.shift_right_logical(lane_r, 2) == lane_c + 1) & (lane_r < 20))

    def read_slots(lo, n):
        meta = slots[lo : lo + n, D:WIDE].astype(F32)
        match = ones_where((meta == (grp + 1).astype(F32)) & (iota((n, 128), 1) < 4))
        chosen = (mm(match, repeat) * meta).astype(BF16)
        return mm(match, first_four), mm(chosen, to_facts).astype(BF16)

    def pack_slots(lo, n, place, facts):
        lane_f = iota((n, 128), 1).astype(F32)
        unpack[lo : lo + n, 0:128] = ones_where(place == lane_f)
        unpack[lo : lo + n, 128:256] = ones_where(place == lane_f + 128.0)
        place_t = lax.dot_general(
            ones_where(iota((8, 128), 1) == 0), place.astype(BF16), NT, preferred_element_type=F32
        )
        pack = ones_where(iota((CAP, n), 0).astype(F32) == place_t[0:1])
        return mm(pack, slots[lo : lo + n, 0:D]), mm(pack, facts)

    live, facts = read_slots(0, BULK)
    live_b = live.astype(BF16)
    place = jnp.where(live > 0, mm(earlier[...], live_b), -1.0)
    bulk_rows, bulk_facts = pack_slots(0, BULK, place, facts)
    bulk_count = mm(ones_where(iota((SLOTS - BULK, BULK), 0) >= 0), live_b)
    place_back(3)
    place_back(4)
    for copy in slots_in[4]:
        copy.wait_recv()
    live, facts = read_slots(BULK, SLOTS - BULK)
    shape = (SLOTS - BULK, SLOTS - BULK)
    place = bulk_count + mm(ones_where(iota(shape, 1) < iota(shape, 0)), live.astype(BF16))
    place = jnp.where(live > 0, place, -1.0)
    last_rows, last_facts = pack_slots(BULK, SLOTS - BULK, place, facts)
    rows[0, 0] = (bulk_rows + last_rows).astype(BF16)
    row_facts[0, 0] = lax.dot_general(
        first_lanes, (bulk_facts + last_facts).astype(BF16), NT, preferred_element_type=F32
    )

    def top(r):
        return pl.ds(r * 128, 128)

    f_up = send(row_facts.at[0, 0], row_facts.at[3, 0], y_next)
    f_down = send(row_facts.at[0, 0], row_facts.at[1, 0], y_prev)
    up, down = [], []
    for r in range(2):
        up.append(send(rows.at[0, 0, top(r)], rows.at[3, 0, top(r)], y_next))
        down.append(send(rows.at[0, 0, top(1 - r)], rows.at[1, 0, top(1 - r)], y_prev))

    def rows_across(i, r):
        return send(rows.at[i, 0, top(r)], rows.at[i, 1, top(r)], twin)

    def facts_across(i):
        return send(row_facts.at[i, 0], row_facts.at[i, 1], twin)

    expert = dev.astype(F32)
    eye_rows = eye(CAP)

    def gains(i):
        for core in range(2):
            f = row_facts[i, core]
            weight = jnp.where(f[0:1] == expert, f[2:3], 0.0) + jnp.where(f[1:2] == expert, f[3:4], 0.0)
            weight = jnp.broadcast_to(weight, (128, CAP)).astype(BF16)
            gain[i, core] = lax.dot_general(eye_rows, weight, NT, preferred_element_type=F32)

    def into_hidden(parts):
        for m, (i, core, r) in enumerate(parts):
            lhs[m * 128 : (m + 1) * 128, :] = rows[i, core, r * 128 : (r + 1) * 128, :]

        def part(n, carry):
            at = pl.ds(pl.multiple_of(n * HIDE, HIDE), HIDE)
            hid[:, at] = jnp.maximum(mm(lhs[...], w1[:, at]), 0.0).astype(BF16)
            return carry

        lax.fori_loop(0, FF // HIDE, part, 0)

    def from_hidden(parts, lo=0):
        def part(n, carry):
            at = pl.ds(pl.multiple_of(n * 256, 256), 256)
            got = mm(hid[lo : lo + len(parts) * 128, :], w2[:, at])
            for m, (i, core, r) in enumerate(parts):
                weight = gain[i, core, r * 128 : (r + 1) * 128, :]
                outs[core, i, r * 128 : (r + 1) * 128, at] = (
                    got[m * 128 : (m + 1) * 128] * jnp.concatenate([weight, weight], axis=1)
                ).astype(BF16)
            return carry

        lax.fori_loop(0, D // 256, part, 0)
        return {
            (i, r): send(outs.at[1, i, top(r)], peer.at[i, top(r)], twin)
            for i, core, r in parts
            if core
        }

    y_ways = {1: (y_next, 3), 2: (y_far, 2), 3: (y_prev, 1)}
    finals = []

    def join_cores(i, r, copy):
        copy.wait_recv()
        rr = slice(r * 128, (r + 1) * 128)
        outs[0, i, rr, :] = (outs[0, i, rr, :].astype(F32) + peer[i, rr, :].astype(F32)).astype(BF16)
        to, there = y_ways[i]
        finals.append(send(outs.at[0, i, top(r)], fin.at[there, top(r)], to))

    def both(*halves):
        return [(i, core, r) for core in (1, 0) for i, r in halves]

    near = both((0, 0), (0, 1))
    early = both((3, 0), (1, 1))
    late = both((3, 1), (1, 0))
    last = both((2, 0), (2, 1))
    waits = [rows_across(0, 0), rows_across(0, 1), facts_across(0)]
    load1.wait()
    load2.wait()
    for copy in waits:
        copy.wait_recv()
    gains(0)
    into_hidden(near)
    near_in = from_hidden(near)
    f_up.wait_recv()
    f_far = send(row_facts.at[3, 0], row_facts.at[2, 0], y_next)
    waits = [facts_across(3)]
    f_down.wait_recv()
    waits.append(facts_across(1))
    up[0].wait_recv()
    far = [send(rows.at[3, 0, top(0)], rows.at[2, 0, top(0)], y_next)]
    waits.append(rows_across(3, 0))
    down[0].wait_recv()
    far.append(send(rows.at[1, 0, top(1)], rows.at[2, 0, top(1)], y_prev))
    waits.append(rows_across(1, 1))
    for copy in waits:
        copy.wait_recv()
    gains(3)
    gains(1)
    into_hidden(early)
    early_in = from_hidden(early)
    up[1].wait_recv()
    waits = [rows_across(3, 1)]
    down[1].wait_recv()
    waits.append(rows_across(1, 0))
    f_far.wait_recv()
    waits.append(facts_across(2))
    for copy in waits:
        copy.wait_recv()
    into_hidden(late)
    for (i, r), copy in early_in.items():
        join_cores(i, r, copy)
    gains(2)
    waits = []
    for r in range(2):
        far[r].wait_recv()
        waits.append(rows_across(2, r))
    late_in = from_hidden(late)
    for copy in waits:
        copy.wait_recv()
    into_hidden(last)
    for (i, r), copy in late_in.items():
        join_cores(i, r, copy)
    last_in = from_hidden(last[:2])
    from_hidden(last[2:], CAP)
    for (i, r), copy in last_in.items():
        join_cores(i, r, copy)
    for copy in near_in.values():
        copy.wait_recv()
    own_sum = outs[0, 0].astype(F32) + peer[0].astype(F32)
    for copy in finals:
        copy.wait_recv()
    sums[...] = (
        own_sum + fin[1].astype(F32) + fin[2].astype(F32) + fin[3].astype(F32)
    ).astype(BF16)

    back_in = {}
    for q in range(len(BATCHES) - 1, -1, -1):
        part = BATCHES[q][2]
        lo = q * NX * QUAD
        got = mm(unpack[lo : lo + NX * part, :], sums[...]).astype(BF16)
        spread[q, 0 : NX * part, :] = got
        back[q, 0:part, :] = got[0:part]
        back_in[q] = [
            send(spread.at[q, pl.ds(i * part, part)], back.at[q, pl.ds(there * part, part)], to)
            for i, to, there in x_ways
        ]

    ready = set()

    def own_part(r, h):
        at = ORDER.index(r)
        q = min(at // 4, 3) if r != 8 else 4
        if q not in ready:
            ready.add(q)
            for copy in back_in[q]:
                copy.wait_recv()
            first, owners, part = BATCHES[q]
            n = owners * TOK
            partial_sum[first * TOK : first * TOK + n, :] = mm(
                select_t[q, 0:n, 0 : NX * part], back[q, 0 : NX * part, :]
            )
        return partial_sum[at * TOK + h * PIECE : at * TOK + (h + 1) * PIECE, :]

    arrived = {}
    for step in range(1, 9):
        current = {}
        for h in range(PIECES):
            part = pl.ds(h * PIECE, PIECE)
            for w, way, to in ((0, -1, z_prev), (1, 1, z_next)):
                if step == 1 and (h < PIECES // 2) != (w == 0):
                    continue
                value = own_part(8 if step == 1 else way * (9 - step), h)
                if (w, h) in arrived:
                    arrived[w, h].wait_recv()
                    value = value + ring_in[w, step - 2, h * PIECE : (h + 1) * PIECE, :].astype(F32)
                ring_out[w, step - 1, h * PIECE : (h + 1) * PIECE, :] = value.astype(BF16)
                current[w, h] = send(ring_out.at[w, step - 1, part], ring_in.at[w, step - 1, part], to)
        arrived = current
    for copy in arrived.values():
        copy.wait_recv()
    out_ref[...] = (
        partial_sum[0:TOK, :] + ring_in[0, 7].astype(F32) + ring_in[1, 7].astype(F32)
    ).astype(BF16)

    for copy in started:
        copy.wait_send()


def per_device(tokens, expert_ids, gates, w_in, w_out):
    vmem = pl.BlockSpec(memory_space=pltpu.VMEM)
    hbm = pl.BlockSpec(memory_space=pl.ANY)
    return pl.pallas_call(
        kernel,
        out_shape=jax.ShapeDtypeStruct((TOK, D), BF16),
        in_specs=[vmem, vmem, vmem, hbm, hbm],
        out_specs=vmem,
        scratch_shapes=[
            pltpu.VMEM((D, FF), BF16),
            pltpu.VMEM((FF, D), BF16),
            pltpu.VMEM((NZ * TOK, WIDE), BF16),
            pltpu.VMEM((5, 8, 256), F32),
            pltpu.VMEM((5, 256, NX * QUAD), BF16),
            pltpu.VMEM((5, NX * QUAD, WIDE), BF16),
            pltpu.VMEM((SLOTS, WIDE), BF16),
            pltpu.VMEM((BULK, BULK), BF16),
            pltpu.VMEM((SLOTS, CAP), BF16),
            pltpu.VMEM((4, CAP, D), BF16),
            pltpu.VMEM((2 * CAP, D), BF16),
            pltpu.VMEM((2 * CAP, FF), BF16),
            pltpu.VMEM((4, 2, CAP, 128), F32),
            pltpu.VMEM((4, 2, CAP, D), BF16),
            pltpu.VMEM((4, 2, 8, CAP), F32),
            pltpu.VMEM((2, 4, CAP, D), BF16),
            pltpu.VMEM((4, CAP, D), BF16),
            pltpu.VMEM((CAP, D), BF16),
            pltpu.VMEM((5, NX * QUAD, D), BF16),
            pltpu.VMEM((5, NX * QUAD, D), BF16),
            pltpu.VMEM((NZ * TOK, D), F32),
            pltpu.VMEM((2, 8, TOK, D), BF16),
            pltpu.VMEM((2, 8, TOK, D), BF16),
            pltpu.SemaphoreType.DMA((2,)),
            pltpu.SemaphoreType.DMA((COPIES,)),
            pltpu.SemaphoreType.DMA((COPIES,)),
        ],
        compiler_params=pltpu.CompilerParams(
            collective_id=0, has_side_effects=True, vmem_limit_bytes=56 * 1024 * 1024
        ),
        cost_estimate=pl.CostEstimate(
            flops=15_000_000_000, bytes_accessed=5_000_000, transcendentals=0
        ),
    )(tokens, expert_ids, gates, w_in, w_out)


def solution(mesh):
    tok = P(("grp", "dev"), None)
    return jax.shard_map(
        per_device,
        mesh=mesh,
        in_specs=(tok, tok, tok, P(("grp", "dev"), None, None), P(("grp", "dev"), None, None)),
        out_specs=tok,
        check_vma=False,
    )
```

time: 133 us -> 124 us (0.932)
  Pallas kernels: 126 us -> 120 us
    pallas_call x1, Pallas kernels: 126 us -> 120 us  [per_device(): pl.pallas_call(kernel, out_shape=jax.ShapeDtypeStruct((TOK, D), BF16), in...]
    unnamed x5 -> x3, local copies, waits for them, and re-layouts: 1.96 us -> 4.29 us
    concatenate x1 -> x0, local copies, waits for them, and re-layouts: 1.63 us -> none  [per_device(): jnp.concatenate([tokens, (pairs[:, :, 0] // 8 + 1).astype(BF16), (pairs[:...]
    slice x2 -> x0, local copies, waits for them, and re-layouts: 1.53 us -> none  [the longest x1 0.77 us: per_device(): pairs[:, :, 1] % 8]
where the time goes in v4:
time: 124 us
  Pallas kernels  120 us (97%)
  local copies, waits for them, and re-layouts  4.29 us (3%)
    pallas_call x1, Pallas kernels, per_device(): pl.pallas_call(kernel, out_shape=jax.ShapeDtypeStruct((TOK, D), BF16), in...  120 us
    unnamed x3, local copies, waits for them, and re-layouts  4.29 us

profile of v4, /device:TPU:6, one launch (start us, length us, event | category | flops | bytes accessed | tf_op | source)
XLA Modules:
  0.0 123.8 jit_solution(11644655891766588644)
XLA Ops:
  0.0 1.4 %copy.7.gates_ref = bf16[64,8]{1,0:T(8,128)(2,1)} copy(bf16[64,8]{0,1:T(8,128)(2,1)} %param.7) | data formatting | bytes 2048 | tf_op args[2]
  1.4 1.4 %copy.6.ids_ref = s32[64,8]{1,0:T(8,128)} copy(s32[64,8]{0,1:T(8,128)} %param.6) | data formatting | bytes 4096 | tf_op args[1]
  2.7 119.5 %shard_map.55 = bf16[64,768]{1,0:T(8,128)(2,1)} custom-call(bf16[64,768]{1,0:T(8,128)(2,1)} %tok_ref.1, s32[64,8]{1,0:T(8,128)} %copy.6.ids_ref, bf16[64,8]{1,0:T(8,128)(2,1)} %copy.7.gates_ref, bf16[1,768,1536]{2,1,0:T(8,128)(2,1)} %w1_hbm.1, bf16[1,1536,768]{2,1,0:T(8,128)(2,1)} %w2_hbm.1), custom_call_target="tpu_custom_call" | custom-call | flops 15000000512 | bytes 5000000 | tf_op jit(solution)/shard_map/pallas_call | solution.py:457
  122.3 1.5 %copy.9 = bf16[64,768]{1,0:T(8,128)(2,1)} copy(bf16[64,768]{1,0:T(8,128)(2,1)} %shard_map.55) | data formatting | bytes 196608

commit v5 on v4

--- a/solution.py
+++ b/solution.py
@@ -97,22 +97,29 @@
     for neighbour in (z_next, z_prev, x_next, x_prev, x_far, y_next, y_prev, y_far, twin):
         pl.semaphore_signal(barrier, inc=1, device_id=neighbour, device_id_type=MESH)
 
+    square_r, square_c = iota((TOK, TOK), 0), iota((TOK, TOK), 1)
+
+    def turned(picks):
+        return lax.dot_general(
+            ones_where(square_r == square_c), picks, NT, preferred_element_type=F32
+        ).astype(BF16)
+
     ids = ids_ref[...]
     to_r, to_c = iota((8, 128), 0), iota((8, 128), 1)
     column[0:TOK, 0:D] = tok_ref[...]
     column[0:TOK, D:WIDE] = (
         mm(
-            (lax.shift_right_logical(ids, 3) + 1).astype(F32).astype(BF16),
+            turned((lax.shift_right_logical(ids, 3) + 1).astype(F32).astype(BF16)),
             ones_where((to_r == 2 * to_c) & (to_c < 4)),
         )
         + mm(
-            jnp.bitwise_and(ids, 7).astype(F32).astype(BF16),
+            turned(jnp.bitwise_and(ids, 7).astype(F32).astype(BF16)),
             ones_where(
                 ((to_r == 2 * (to_c - 4)) & (to_c < 8)) | ((to_r == 2 * (to_c - 8) + 1) & (to_c < 12))
             ),
         )
         + mm(
-            gates_ref[...],
+            turned(gates_ref[...]),
             ones_where(
                 ((to_r == 2 * (to_c - 12)) & (to_c < 16)) | ((to_r == 2 * (to_c - 16) + 1) & (to_c < 20))
             ),
@@ -121,9 +128,10 @@
     pl.semaphore_wait(barrier, 9)
 
     started = []
+    numbers = iter(range(COPIES))
 
     def send(src, dst, to):
-        k = len(started)
+        k = next(numbers)
         copy = pltpu.make_async_remote_copy(
             src_ref=src,
             dst_ref=dst,
@@ -272,9 +280,12 @@
     f_up = send(row_facts.at[0, 0], row_facts.at[3, 0], y_next)
     f_down = send(row_facts.at[0, 0], row_facts.at[1, 0], y_prev)
     up, down = [], []
-    for r in range(2):
+
+    def along_y(r):
         up.append(send(rows.at[0, 0, top(r)], rows.at[3, 0, top(r)], y_next))
         down.append(send(rows.at[0, 0, top(1 - r)], rows.at[1, 0, top(1 - r)], y_prev))
+
+    along_y(0)
 
     def rows_across(i, r):
         return send(rows.at[i, 0, top(r)], rows.at[i, 1, top(r)], twin)
@@ -345,12 +356,21 @@
         copy.wait_recv()
     gains(0)
     into_hidden(near)
+    for copy in (up[0], down[0]):
+        copy.wait_send()
+        started[:] = [other for other in started if other is not copy]
+    along_y(1)
     near_in = from_hidden(near)
     f_up.wait_recv()
     f_far = send(row_facts.at[3, 0], row_facts.at[2, 0], y_next)
     waits = [facts_across(3)]
     f_down.wait_recv()
     waits.append(facts_across(1))
+    for copy in waits:
+        copy.wait_recv()
+    gains(3)
+    gains(1)
+    waits = []
     up[0].wait_recv()
     far = [send(rows.at[3, 0, top(0)], rows.at[2, 0, top(0)], y_next)]
     waits.append(rows_across(3, 0))
@@ -359,8 +379,6 @@
     waits.append(rows_across(1, 1))
     for copy in waits:
         copy.wait_recv()
-    gains(3)
-    gains(1)
     into_hidden(early)
     early_in = from_hidden(early)
     up[1].wait_recv()
@@ -399,7 +417,8 @@
     ).astype(BF16)
 
     back_in = {}
-    for q in range(len(BATCHES) - 1, -1, -1):
+
+    def along_x(q):
         part = BATCHES[q][2]
         lo = q * NX * QUAD
         got = mm(unpack[lo : lo + NX * part, :], sums[...]).astype(BF16)
@@ -410,6 +429,8 @@
             for i, to, there in x_ways
         ]
 
+    along_x(4)
+    along_x(3)
     ready = set()
 
     def own_part(r, h):
@@ -441,6 +462,8 @@
                 ring_out[w, step - 1, h * PIECE : (h + 1) * PIECE, :] = value.astype(BF16)
                 current[w, h] = send(ring_out.at[w, step - 1, part], ring_in.at[w, step - 1, part], to)
         arrived = current
+        if step in (1, 2, 4):
+            along_x({1: 2, 2: 1, 4: 0}[step])
     for copy in arrived.values():
         copy.wait_recv()
     out_ref[...] = (
@@ -493,7 +516,7 @@
         cost_estimate=pl.CostEstimate(
             flops=15_000_000_000, bytes_accessed=5_000_000, transcendentals=0
         ),
-    )(tokens, expert_ids, gates, w_in, w_out)
+    )(tokens, expert_ids.T, gates.T, w_in, w_out)
 
 
 def solution(mesh):

time: 124 us -> 122 us (0.984)
  local copies, waits for them, and re-layouts: 4.29 us -> 1.54 us
    unnamed x3 -> x1, local copies, waits for them, and re-layouts: 4.29 us -> 1.54 us
where the time goes in v5:
time: 122 us; the launch traced here: 121 us
  Pallas kernels  120 us (98%)
  local copies, waits for them, and re-layouts  1.54 us (1%)
    pallas_call x1, Pallas kernels, per_device(): pl.pallas_call(kernel, out_shape=jax.ShapeDtypeStruct((TOK, D), BF16), in...  120 us

profile of v5, /device:TPU:6, one launch (start us, length us, event | category | flops | bytes accessed | tf_op | source)
XLA Modules:
  0.0 121.4 jit_solution(13632486470643329336)
XLA Ops:
  0.0 119.9 %shard_map.55 = bf16[64,768]{1,0:T(8,128)(2,1)} custom-call(bf16[64,768]{1,0:T(8,128)(2,1)} %tok_ref.1, s32[8,64]{1,0:T(8,128)} %bitcast.2, bf16[8,64]{1,0:T(8,128)(2,1)} %bitcast.3, bf16[1,768,1536]{2,1,0:T(8,128)(2,1)} %w1_hbm.1, bf16[1,1536,768]{2,1,0:T(8,128)(2,1)} %w2_hbm.1), custom_call_target="tpu_custom_call" | custom-call | flops 15000000512 | bytes 5000000 | tf_op jit(solution)/shard_map/pallas_call | solution.py:480
  119.9 1.5 %copy.7 = bf16[64,768]{1,0:T(8,128)(2,1)} copy(bf16[64,768]{1,0:T(8,128)(2,1)} %shard_map.55) | data formatting | bytes 196608

commit v6 on v5

--- a/solution.py
+++ b/solution.py
@@ -286,6 +286,7 @@
         down.append(send(rows.at[0, 0, top(1 - r)], rows.at[1, 0, top(1 - r)], y_prev))
 
     along_y(0)
+    along_y(1)
 
     def rows_across(i, r):
         return send(rows.at[i, 0, top(r)], rows.at[i, 1, top(r)], twin)
@@ -356,10 +357,6 @@
         copy.wait_recv()
     gains(0)
     into_hidden(near)
-    for copy in (up[0], down[0]):
-        copy.wait_send()
-        started[:] = [other for other in started if other is not copy]
-    along_y(1)
     near_in = from_hidden(near)
     f_up.wait_recv()
     f_far = send(row_facts.at[3, 0], row_facts.at[2, 0], y_next)
@@ -389,9 +386,9 @@
     waits.append(facts_across(2))
     for copy in waits:
         copy.wait_recv()
-    into_hidden(late)
     for (i, r), copy in early_in.items():
         join_cores(i, r, copy)
+    into_hidden(late)
     gains(2)
     waits = []
     for r in range(2):
@@ -400,11 +397,10 @@
     late_in = from_hidden(late)
     for copy in waits:
         copy.wait_recv()
-    into_hidden(last)
     for (i, r), copy in late_in.items():
         join_cores(i, r, copy)
-    last_in = from_hidden(last[:2])
-    from_hidden(last[2:], CAP)
+    into_hidden(last)
+    last_in = from_hidden(last)
     for (i, r), copy in last_in.items():
         join_cores(i, r, copy)
     for copy in near_in.values():
@@ -429,8 +425,8 @@
             for i, to, there in x_ways
         ]
 
-    along_x(4)
-    along_x(3)
+    for q in (4, 3, 2, 1, 0):
+        along_x(q)
     ready = set()
 
     def own_part(r, h):
@@ -462,13 +458,11 @@
                 ring_out[w, step - 1, h * PIECE : (h + 1) * PIECE, :] = value.astype(BF16)
                 current[w, h] = send(ring_out.at[w, step - 1, part], ring_in.at[w, step - 1, part], to)
         arrived = current
-        if step in (1, 2, 4):
-            along_x({1: 2, 2: 1, 4: 0}[step])
     for copy in arrived.values():
         copy.wait_recv()
     out_ref[...] = (
         partial_sum[0:TOK, :] + ring_in[0, 7].astype(F32) + ring_in[1, 7].astype(F32)
-    ).astype(BF16)
+    )
 
     for copy in started:
         copy.wait_send()
@@ -479,7 +473,7 @@
     hbm = pl.BlockSpec(memory_space=pl.ANY)
     return pl.pallas_call(
         kernel,
-        out_shape=jax.ShapeDtypeStruct((TOK, D), BF16),
+        out_shape=jax.ShapeDtypeStruct((TOK, D), F32),
         in_specs=[vmem, vmem, vmem, hbm, hbm],
         out_specs=vmem,
         scratch_shapes=[
@@ -516,7 +510,7 @@
         cost_estimate=pl.CostEstimate(
             flops=15_000_000_000, bytes_accessed=5_000_000, transcendentals=0
         ),
-    )(tokens, expert_ids.T, gates.T, w_in, w_out)
+    )(tokens, expert_ids.T, gates.T, w_in, w_out).astype(BF16)
 
 
 def solution(mesh):

time: 122 us -> 122 us (level)
  other arithmetic: 0 us -> 1.58 us
  local copies, waits for them, and re-layouts: 1.54 us -> 0 us
    convert_element_type x0 -> x1, other arithmetic: none -> 1.58 us  [per_device(): return pl.pallas_call(kernel, out_shape=jax.ShapeDtypeStruct((TOK, D), F3...]
    unnamed x1 -> x0, local copies, waits for them, and re-layouts: 1.54 us -> none
where the time goes in v6:
time: 122 us; the launch traced here: 121 us
  Pallas kernels  120 us (98%)
  other arithmetic  1.58 us (1%)
    pallas_call x1, Pallas kernels, per_device(): pl.pallas_call(kernel, out_shape=jax.ShapeDtypeStruct((TOK, D), F32), in_...  120 us

profile of v6, /device:TPU:6, one launch (start us, length us, event | category | flops | bytes accessed | tf_op | source)
XLA Modules:
  0.0 121.1 jit_solution(11902413200511471942)
XLA Ops:
  0.0 119.5 %shard_map.55 = f32[64,768]{1,0:T(8,128)} custom-call(bf16[64,768]{1,0:T(8,128)(2,1)} %tok_ref.1, s32[8,64]{1,0:T(8,128)} %bitcast.2, bf16[8,64]{1,0:T(8,128)(2,1)} %bitcast.3, bf16[1,768,1536]{2,1,0:T(8,128)(2,1)} %w1_hbm.1, bf16[1,1536,768]{2,1,0:T(8,128)(2,1)} %w2_hbm.1), custom_call_target="tpu_custom_call" | custom-call | flops 15000000512 | bytes 5000000 | tf_op jit(solution)/shard_map/pallas_call | solution.py:474
  119.5 1.6 %convert_element_type.3 = bf16[64,768]{1,0:T(8,128)(2,1)} convert(f32[64,768]{1,0:T(8,128)} %shard_map.55) | non-fusion elementwise | flops 49152 | bytes 294912 | tf_op jit(solution)/shard_map/convert_element_type | solution.py:513

commit v7 on v6

--- a/solution.py
+++ b/solution.py
@@ -227,9 +227,6 @@
         if step in (3, 5, 7, 8, 9):
             q = (3, 5, 7, 8, 9).index(step)
             slots_in[q] = place_batch(q)
-        if step in (4, 6):
-            place_back(step // 2 - 2)
-    place_back(2)
     for q in range(4):
         for copy in slots_in[q]:
             copy.wait_recv()
@@ -260,8 +257,6 @@
     place = jnp.where(live > 0, mm(earlier[...], live_b), -1.0)
     bulk_rows, bulk_facts = pack_slots(0, BULK, place, facts)
     bulk_count = mm(ones_where(iota((SLOTS - BULK, BULK), 0) >= 0), live_b)
-    place_back(3)
-    place_back(4)
     for copy in slots_in[4]:
         copy.wait_recv()
     live, facts = read_slots(BULK, SLOTS - BULK)
@@ -367,6 +362,8 @@
         copy.wait_recv()
     gains(3)
     gains(1)
+    for q in range(len(BATCHES)):
+        place_back(q)
     waits = []
     up[0].wait_recv()
     far = [send(rows.at[3, 0, top(0)], rows.at[2, 0, top(0)], y_next)]

time: 122 us -> 123 us (level)
  no operation moved by 1% of the time
where the time goes in v7:
time: 123 us; the launch traced here: 122 us
  Pallas kernels  121 us (98%)
  other arithmetic  1.58 us (1%)
    pallas_call x1, Pallas kernels, per_device(): pl.pallas_call(kernel, out_shape=jax.ShapeDtypeStruct((TOK, D), F32), in_...  121 us

profile of v7, /device:TPU:6, one launch (start us, length us, event | category | flops | bytes accessed | tf_op | source)
XLA Modules:
  0.0 122.2 jit_solution(1064991294487886784)
XLA Ops:
  0.0 120.6 %shard_map.55 = f32[64,768]{1,0:T(8,128)} custom-call(bf16[64,768]{1,0:T(8,128)(2,1)} %tok_ref.1, s32[8,64]{1,0:T(8,128)} %bitcast.2, bf16[8,64]{1,0:T(8,128)(2,1)} %bitcast.3, bf16[1,768,1536]{2,1,0:T(8,128)(2,1)} %w1_hbm.1, bf16[1,1536,768]{2,1,0:T(8,128)(2,1)} %w2_hbm.1), custom_call_target="tpu_custom_call" | custom-call | flops 15000000512 | bytes 5000000 | tf_op jit(solution)/shard_map/pallas_call | solution.py:471
  120.7 1.6 %convert_element_type.3 = bf16[64,768]{1,0:T(8,128)(2,1)} convert(f32[64,768]{1,0:T(8,128)} %shard_map.55) | non-fusion elementwise | flops 49152 | bytes 294912 | tf_op jit(solution)/shard_map/convert_element_type | solution.py:510
